TPU v7x, 32 devices: a whole 2x2x4 slice. The times are simulated.
32 devices in a mesh: lat: 8 (over y, x, core), lon: 4 (over z).
Axes of the slice: x: 2, y: 2, z: 4, core: 2. Of those that a mesh axis runs over, the one named last changes fastest.
Arguments:
- potential_heat_state: float32 [16, 512, 512], P(None, 'lat', 'lon'), may hold values from -6 to 6
- saltiness_anomaly: float32 [16, 512, 512], P(None, 'lat', 'lon'), may hold values from -6 to 6
- first_current_component: float32 [16, 512, 512], P(None, 'lat', 'lon'), may hold values from -6 to 6
- second_current_component: float32 [16, 512, 512], P(None, 'lat', 'lon'), may hold values from -6 to 6
- bathymetry_layer_total: int32 [512, 512], P('lat', 'lon'), may hold values from 0 to 16
- westeast_cell_extent: float32 [512, 512], P('lat', 'lon'), may hold values from 1 to 2
- southnorth_cell_extent: float32 [512, 512], P('lat', 'lon'), may hold values from 1 to 2
- planetary_vorticity: float32 [512, 512], P('lat', 'lon'), may hold values from -1.5 to 1.5
- scalar_mixing_factor: float32 [16], replicated, may hold values from 0.05 to 0.5
- momentum_mixing_factor: float32 [16], replicated, may hold values from 0.05 to 0.5
Outputs:
- new_temperature: float32 [16, 512, 512], P(None, 'lat', 'lon')
- new_salinity: float32 [16, 512, 512], P(None, 'lat', 'lon')
- new_zonal: float32 [16, 512, 512], P(None, 'lat', 'lon')
- new_north: float32 [16, 512, 512], P(None, 'lat', 'lon')
All inputs are finite; a program needn't handle non-finite values.
Results may differ from a plain program's by a relative error of at most 0.00002.
Values sent between devices are 32-bit elements; how exact they have to be, the bound alone decides.
A program may use at most 64 MiB of HBM per device.

v0:
```python
import jax
import jax.numpy as jnp
from jax import lax
from jax.sharding import PartitionSpec as P

STEPS = 3


time_step = 0.2


def partner(value, axis, apart):
    mask = 2**apart
    pairs = [(source, source ^ mask) for source in range(lax.axis_size(axis))]
    return lax.ppermute(value, axis, pairs)


def with_halo(value, sides, width, wrap):
    for axis, dim in sides:
        peers, length = (lax.axis_size(axis), value.shape[dim])
        up = [(i, (i + 1) % peers) for i in range(peers if wrap else peers - 1)]
        down = [(j, i) for i, j in up]
        last = lax.slice_in_dim(value, length - width, length, axis=dim)
        initial = lax.slice_in_dim(value, 0, width, axis=dim)
        before = lax.ppermute(last, axis, up)
        after = lax.ppermute(initial, axis, down)
        value = jnp.concatenate([before, value, after], axis=dim)
    return value


def tendency(
    extended, prognostic_quantities, inv_width, inv_height, planetary_vorticity, diffusion
):
    east_side = extended[:, :, 1:-1, 2:]
    west_side = extended[:, :, 1:-1, :-2]
    north_side = extended[:, :, 2:, 1:-1]
    south_side = extended[:, :, :-2, 1:-1]
    grad_east = (east_side - west_side) * 0.5 * inv_width
    grad_north = (north_side - south_side) * 0.5 * inv_height
    laplace = (east_side + west_side - 2.0 * prognostic_quantities) * (inv_width * inv_width) + (
        north_side + south_side - 2.0 * prognostic_quantities
    ) * (inv_height * inv_height)
    zonal_mid = prognostic_quantities[2]
    north_mid = prognostic_quantities[3]
    advection = -(zonal_mid[None] * grad_east + north_mid[None] * grad_north)
    zeros_plane = jnp.zeros_like(zonal_mid)
    rotation = jnp.stack(
        [
            zeros_plane,
            zeros_plane,
            planetary_vorticity * north_mid,
            -planetary_vorticity * zonal_mid,
        ]
    )
    return advection + diffusion * laplace + rotation


def mirror_row(edge_row):
    moved = edge_row
    for bit_index in range(lax.axis_size("lon").bit_length() - 1):
        moved = partner(moved, "lon", bit_index)
    return moved[..., ::-1]


def field_rims(prognostic_quantities, rim_depth):
    padded = with_halo(prognostic_quantities, (("lat", 2),), rim_depth, False)
    return with_halo(padded, (("lon", 3),), rim_depth, True)


def on_device(
    potential_heat_state,
    saltiness_anomaly,
    first_current_component,
    second_current_component,
    bathymetry_layer_total,
    westeast_cell_extent,
    southnorth_cell_extent,
    planetary_vorticity,
    scalar_mixing_factor,
    momentum_mixing_factor,
):
    layered_columns = potential_heat_state.shape[0]
    partition_strips = potential_heat_state.shape[1]
    rim_depth = 1
    own_index = lax.broadcasted_iota(
        jnp.int32, (layered_columns,) + bathymetry_layer_total.shape, 0
    )
    local_mask = (own_index < bathymetry_layer_total[None]).astype(jnp.float32)
    prognostic_quantities = (
        jnp.stack(
            [
                potential_heat_state,
                saltiness_anomaly,
                first_current_component,
                second_current_component,
            ]
        )
        * local_mask[None]
    )
    fold_signs = jnp.array([1.0, 1.0, -1.0, -1.0], jnp.float32).reshape(4, 1, 1)
    diffusion = jnp.stack(
        [scalar_mixing_factor, scalar_mixing_factor, momentum_mixing_factor, momentum_mixing_factor]
    )[:, :, None, None]
    on_fold = lax.axis_index("lat") == lax.axis_size("lat") - 1
    ghost_index = rim_depth + partition_strips
    inv_width = 1.0 / westeast_cell_extent
    inv_height = 1.0 / southnorth_cell_extent
    for substep in range(STEPS):
        extended = field_rims(prognostic_quantities, rim_depth)
        ghost_row = fold_signs * mirror_row(extended[:, :, ghost_index - 1, :])
        upper_row = jnp.where(on_fold, ghost_row, extended[:, :, ghost_index, :])
        extended = extended.at[:, :, ghost_index, :].set(upper_row)
        middle = extended[:, :, 1:-1, 1:-1]
        change = tendency(extended, middle, inv_width, inv_height, planetary_vorticity, diffusion)
        updated = middle + time_step * local_mask[None] * change
        extended = extended.at[:, :, 1:-1, 1:-1].set(updated)
        prognostic_quantities = extended[:, :, 1:-1, 1:-1]
    return (
        prognostic_quantities[0],
        prognostic_quantities[1],
        prognostic_quantities[2],
        prognostic_quantities[3],
    )


def solution(mesh):
    placed = (
        P(None, "lat", "lon"),
        P(None, "lat", "lon"),
        P(None, "lat", "lon"),
        P(None, "lat", "lon"),
        P("lat", "lon"),
        P("lat", "lon"),
        P("lat", "lon"),
        P("lat", "lon"),
        P(),
        P(),
    )
    return jax.shard_map(
        on_device,
        mesh=mesh,
        in_specs=placed,
        out_specs=(
            P(None, "lat", "lon"),
            P(None, "lat", "lon"),
            P(None, "lat", "lon"),
            P(None, "lat", "lon"),
        ),
        check_vma=False,
    )
```

profile of v0, /device:TPU:0, one launch (start us, length us, event | category | flops | bytes accessed | tf_op | source)
XLA Modules:
  0.0 179.3 jit_solution(13935013116927063288)
XLA Ops:
  0.7 0.9 fusion.7
  1.5 1.8 %copy_bitcast_fusion.2 = (f32[1,16,64,128]{3,1,0,2:T(8,128)S(1)}, f32[1,16,64,128]{3,1,0,2:T(8,128)S(1)}) fusion(f32[16,64,128]{2,1,0:T(8,128)} %param.24, f32[16,64,128]{2,1,0:T(8,128)} %param.23), kind=kLoop, calls=%fused_computation.22 | loop fusion | bytes 2097152 | tf_op jit(solution)/shard_map/stack | solution.py:90
  3.4 0.6 copy_bitcast_fusion
  4.0 0.2 maximum_multiply_fusion
  4.2 2.4 %collective-permute-start = (f32[4,16,1,128]{3,1,0,2:T(8,128)S(1)}, f32[4,16,1,128]{3,1,0,2:T(8,128)S(1)}, u32[]{:S(2)}, u32[]{:S(2)}) collective-permute-start(f32[4,16,1,128]{3,1,0,2:T(8,128)S(1)} %get-tuple-element.110), channel_id=1, source_target_pairs={{0,4},{4,8},{8,12},{12,16},{16,20},{20,24},{24,28},{1,5},{5,9},{9,... | collective-permute-start | bytes 98312 | tf_op jit(solution)/shard_map/ppermute | solution.py:25
  6.6 1.3 collective-permute-start.1
  7.9 3.9 %collective-permute-done.1 = f32[4,16,1,128]{3,1,0,2:T(8,128)S(1)} collective-permute-done((f32[4,16,1,128]{3,1,0,2:T(8,128)S(1)}, f32[4,16,1,128]{3,1,0,2:T(8,128)S(1)}, u32[]{:S(2)}, u32[]{:S(2)}) %collective-permute-start.1) | collective-permute-done | bytes 32800 | tf_op jit(solution)/shard_map/ppermute | solution.py:26
  11.8 0.2 pad_maximum_fusion.3
  12.1 2.8 %fusion.21 = (f32[4,16,66,1]{3,1,0,2:T(8,128)}, f32[4,16,66,1]{3,1,0,2:T(8,128)}) fusion(f32[4,16,66,128]{3,1,0,2:T(8,128)S(1)} %pad_maximum_fusion.3), kind=kLoop, calls=%fused_computation.63 | loop fusion | bytes 67584 | tf_op jit(solution)/shard_map/slice | solution.py:23
  14.9 2.8 %copy.72 = f32[4,16,66,1]{2,1,3,0:T(8,128)S(1)} copy(f32[4,16,66,1]{3,1,0,2:T(8,128)} %get-tuple-element.100) | data formatting | bytes 33792 | tf_op jit(solution)/shard_map/slice | solution.py:23
  17.7 2.8 %copy.73 = f32[4,16,66,1]{2,1,3,0:T(8,128)S(1)} copy(f32[4,16,66,1]{3,1,0,2:T(8,128)} %get-tuple-element.101) | data formatting | bytes 33792 | tf_op jit(solution)/shard_map/slice | solution.py:24
  20.4 3.6 %collective-permute-start.3 = (f32[4,16,66,1]{2,1,3,0:T(8,128)S(1)}, f32[4,16,66,1]{2,1,3,0:T(8,128)S(1)}, u32[]{:S(2)}, u32[]{:S(2)}) collective-permute-start(f32[4,16,66,1]{2,1,3,0:T(8,128)S(1)} %copy.73), channel_id=1, source_target_pairs={{1,0},{2,1},{3,2},{0,3},{5,4},{6,5},{7,6},{4,7},{9,8},{10,9},{11,1... | collective-permute-start | bytes 50696 | tf_op jit(solution)/shard_map/ppermute | solution.py:26
  24.1 5.6 %collective-permute-done.2 = f32[4,16,66,1]{2,1,3,0:T(8,128)S(1)} collective-permute-done((f32[4,16,66,1]{2,1,3,0:T(8,128)S(1)}, f32[4,16,66,1]{2,1,3,0:T(8,128)S(1)}, u32[]{:S(2)}, u32[]{:S(2)}) %collective-permute-start.2) | collective-permute-done | bytes 16928 | tf_op jit(solution)/shard_map/ppermute | solution.py:25
  29.8 3.1 %copy.74 = f32[4,16,66,1]{3,1,0,2:T(8,128)} copy(f32[4,16,66,1]{2,1,3,0:T(8,128)S(1)} %collective-permute-done.2) | data formatting | bytes 33792 | tf_op jit(solution)/shard_map/ppermute | solution.py:25
  32.8 3.1 %copy.75 = f32[4,16,66,1]{3,1,0,2:T(8,128)} copy(f32[4,16,66,1]{2,1,3,0:T(8,128)S(1)} %collective-permute-done.3) | data formatting | bytes 33792 | tf_op jit(solution)/shard_map/ppermute | solution.py:26
  35.9 4.1 %pad_maximum_fusion = f32[4,16,66,130]{3,1,0,2:T(8,128)S(1)} fusion(f32[4,16,66,1]{3,1,0,2:T(8,128)} %copy.75, f32[4,16,1,128]{3,1,0,2:T(8,128)S(1)} %collective-permute-done.1, f32[4,16,64,128]{3,1,0,2:T(8,128)S(1)} %maximum_multiply_fusion, f32[4,16,1,128]{3,1,0,2:T(8,128)S(1)} %collective-permute-done, f32[4,16,66,1]{3,1,0,2:T(8,128)} %copy.74), kind=kLoop, calls=%fused_computation | loop fusion | flops 2196480 | bytes 4392960 | tf_op jit(solution)/shard_map/concatenate | solution.py:27
  40.0 2.0 %copy-done = f32[4,16,66,130]{3,1,0,2:T(8,128)} copy-done((f32[4,16,66,130]{3,1,0,2:T(8,128)}, f32[4,16,66,130]{3,1,0,2:T(8,128)S(1)}, u32[]{:S(2)}) %copy-start) | copy-done | bytes 2196504
  42.0 4.7 %collective-permute-done.4 = f32[4,16,130]{2,1,0:T(8,128)S(1)} collective-permute-done((f32[4,16,130]{2,1,0:T(8,128)S(1)}, f32[4,16,130]{2,1,0:T(8,128)S(1)}, u32[]{:S(2)}, u32[]{:S(2)}) %collective-permute-start.4) | collective-permute-done | bytes 33312 | tf_op jit(solution)/shard_map/ppermute | solution.py:15
  46.8 5.7 %collective-permute-done.5 = f32[4,16,130]{2,1,0:T(8,128)S(1)} collective-permute-done((f32[4,16,130]{2,1,0:T(8,128)S(1)}, f32[4,16,130]{2,1,0:T(8,128)S(1)}, u32[]{:S(2)}, u32[]{:S(2)}) %collective-permute-start.5) | collective-permute-done | bytes 33312 | tf_op jit(solution)/shard_map/ppermute | solution.py:15
  52.7 1.6 fusion.16
  54.2 1.9 %slice_bitcast_fusion.9 = (f32[16,64,128]{2,0,1:T(8,128)S(1)}, f32[1,16,64,128]{3,1,0,2:T(8,128)S(1)}, f32[1,16,64,128]{3,1,0,2:T(8,128)S(1)}, f32[16,64,128]{2,0,1:T(8,128)S(1)}) fusion(f32[4,16,66,130]{3,1,0,2:T(8,128)} %fusion.16, f32[64,128]{1,0:T(8,128)S(1)} %neg.15, f32[64,128]{1,0:T(8,128)S(1)} %copy-done.3), kind=kLoop, calls=%fused_computation.38 | loop fusion | flops 262144 | bytes 3211264 | tf_op jit(solution)/shard_map/mul | solution.py:45
  56.1 8.6 %fusion.1 = f32[4,16,64,128]{3,1,0,2:T(8,128)S(1)} fusion(f32[1,16,64,128]{3,1,0,2:T(8,128)S(1)} %get-tuple-element.93, f32[1,16,64,128]{3,1,0,2:T(8,128)S(1)} %get-tuple-element.94, f32[4,16,66,130]{3,1,0,2:T(8,128)} %fusion.16, f32[4]{0:T(128)S(1)} %pad.40.clone, f32[64,128]{1,0:T(8,128)S(1)} %get-tuple-element.115, f32[64,128]{1,0:T(8,128)S(1)} %get-tuple-element.120, ...), kind=kLoop, calls=%fused_computation.9 | loop fusion | flops 12058624 | bytes 15335696 | tf_op jit(solution)/shard_map/add | solution.py:115
  64.7 1.9 %collective-permute-start.6 = (f32[4,16,1,128]{3,1,0,2:T(8,128)S(1)}, f32[4,16,1,128]{3,1,0,2:T(8,128)S(1)}, u32[]{:S(2)}, u32[]{:S(2)}) collective-permute-start(f32[4,16,1,128]{3,1,0,2:T(8,128)S(1)} %get-tuple-element.108), channel_id=1, source_target_pairs={{0,4},{4,8},{8,12},{12,16},{16,20},{20,24},{24,28},{1,5},{5,9},{9,... | collective-permute-start | bytes 98312 | tf_op jit(solution)/shard_map/ppermute | solution.py:25
  66.7 1.5 collective-permute-start.7
  68.2 3.8 %collective-permute-done.7 = f32[4,16,1,128]{3,1,0,2:T(8,128)S(1)} collective-permute-done((f32[4,16,1,128]{3,1,0,2:T(8,128)S(1)}, f32[4,16,1,128]{3,1,0,2:T(8,128)S(1)}, u32[]{:S(2)}, u32[]{:S(2)}) %collective-permute-start.7) | collective-permute-done | bytes 32800 | tf_op jit(solution)/shard_map/ppermute | solution.py:26
  71.9 0.2 pad_maximum_fusion.4
  72.2 2.8 %fusion.20 = (f32[4,16,66,1]{3,1,0,2:T(8,128)}, f32[4,16,66,1]{3,1,0,2:T(8,128)}) fusion(f32[4,16,66,128]{3,1,0,2:T(8,128)S(1)} %pad_maximum_fusion.4), kind=kLoop, calls=%fused_computation.62 | loop fusion | bytes 67584 | tf_op jit(solution)/shard_map/slice | solution.py:23
  75.0 2.8 %copy.76 = f32[4,16,66,1]{2,1,3,0:T(8,128)S(1)} copy(f32[4,16,66,1]{3,1,0,2:T(8,128)} %get-tuple-element.98) | data formatting | bytes 33792 | tf_op jit(solution)/shard_map/slice | solution.py:23
  77.8 2.8 %copy.77 = f32[4,16,66,1]{2,1,3,0:T(8,128)S(1)} copy(f32[4,16,66,1]{3,1,0,2:T(8,128)} %get-tuple-element.99) | data formatting | bytes 33792 | tf_op jit(solution)/shard_map/slice | solution.py:24
  80.6 3.8 %collective-permute-start.9 = (f32[4,16,66,1]{2,1,3,0:T(8,128)S(1)}, f32[4,16,66,1]{2,1,3,0:T(8,128)S(1)}, u32[]{:S(2)}, u32[]{:S(2)}) collective-permute-start(f32[4,16,66,1]{2,1,3,0:T(8,128)S(1)} %copy.77), channel_id=1, source_target_pairs={{1,0},{2,1},{3,2},{0,3},{5,4},{6,5},{7,6},{4,7},{9,8},{10,9},{11,1... | collective-permute-start | bytes 50696 | tf_op jit(solution)/shard_map/ppermute | solution.py:26
  84.4 3.1 %copy.78 = f32[4,16,66,1]{3,1,0,2:T(8,128)} copy(f32[4,16,66,1]{2,1,3,0:T(8,128)S(1)} %collective-permute-done.8) | data formatting | bytes 33792 | tf_op jit(solution)/shard_map/ppermute | solution.py:25
  87.4 3.1 %copy.79 = f32[4,16,66,1]{3,1,0,2:T(8,128)} copy(f32[4,16,66,1]{2,1,3,0:T(8,128)S(1)} %collective-permute-done.9) | data formatting | bytes 33792 | tf_op jit(solution)/shard_map/ppermute | solution.py:26
  90.5 4.0 %pad_maximum_fusion.1 = f32[4,16,66,130]{3,1,0,2:T(8,128)S(1)} fusion(f32[4,16,66,1]{3,1,0,2:T(8,128)} %copy.79, f32[4,16,1,128]{3,1,0,2:T(8,128)S(1)} %collective-permute-done.7, f32[4,16,64,128]{3,1,0,2:T(8,128)S(1)} %fusion.1, f32[4,16,1,128]{3,1,0,2:T(8,128)S(1)} %collective-permute-done.6, f32[4,16,66,1]{3,1,0,2:T(8,128)} %copy.78), kind=kLoop, calls=%fused_computation.1 | loop fusion | flops 2196480 | bytes 4392960 | tf_op jit(solution)/shard_map/concatenate | solution.py:27
  94.5 2.0 %copy-done.2 = f32[4,16,66,130]{3,1,0,2:T(8,128)} copy-done((f32[4,16,66,130]{3,1,0,2:T(8,128)}, f32[4,16,66,130]{3,1,0,2:T(8,128)S(1)}, u32[]{:S(2)}) %copy-start.2) | copy-done | bytes 2196504
  96.5 4.3 %collective-permute-done.10 = f32[4,16,130]{2,1,0:T(8,128)S(1)} collective-permute-done((f32[4,16,130]{2,1,0:T(8,128)S(1)}, f32[4,16,130]{2,1,0:T(8,128)S(1)}, u32[]{:S(2)}, u32[]{:S(2)}) %collective-permute-start.10) | collective-permute-done | bytes 33312 | tf_op jit(solution)/shard_map/ppermute | solution.py:15
  100.8 1.4 collective-permute-start.11
  102.2 5.5 %collective-permute-done.11 = f32[4,16,130]{2,1,0:T(8,128)S(1)} collective-permute-done((f32[4,16,130]{2,1,0:T(8,128)S(1)}, f32[4,16,130]{2,1,0:T(8,128)S(1)}, u32[]{:S(2)}, u32[]{:S(2)}) %collective-permute-start.11) | collective-permute-done | bytes 33312 | tf_op jit(solution)/shard_map/ppermute | solution.py:15
  107.9 1.6 fusion.13
  109.4 1.9 %slice_bitcast_fusion.7 = (f32[16,64,128]{2,0,1:T(8,128)S(1)}, f32[1,16,64,128]{3,1,0,2:T(8,128)S(1)}, f32[1,16,64,128]{3,1,0,2:T(8,128)S(1)}, f32[16,64,128]{2,0,1:T(8,128)S(1)}) fusion(f32[4,16,66,130]{3,1,0,2:T(8,128)} %fusion.13, f32[64,128]{1,0:T(8,128)S(1)} %neg.15, f32[64,128]{1,0:T(8,128)S(1)} %copy-done.3), kind=kLoop, calls=%fused_computation.34 | loop fusion | flops 262144 | bytes 3211264 | tf_op jit(solution)/shard_map/mul | solution.py:45
  111.3 8.6 %fusion.3 = f32[4,16,64,128]{3,1,0,2:T(8,128)S(1)} fusion(f32[1,16,64,128]{3,1,0,2:T(8,128)S(1)} %get-tuple-element.89, f32[1,16,64,128]{3,1,0,2:T(8,128)S(1)} %get-tuple-element.90, f32[4,16,66,130]{3,1,0,2:T(8,128)} %fusion.13, f32[4]{0:T(128)S(1)} %pad.40.clone, f32[16,64,128]{2,0,1:T(8,128)S(1)} %get-tuple-element.91, ...), kind=kLoop, calls=%fused_computation.12 | loop fusion | flops 12058624 | bytes 15335696 | tf_op jit(solution)/shard_map/add | solution.py:115
  119.9 2.0 %collective-permute-start.12 = (f32[4,16,1,128]{3,1,0,2:T(8,128)S(1)}, f32[4,16,1,128]{3,1,0,2:T(8,128)S(1)}, u32[]{:S(2)}, u32[]{:S(2)}) collective-permute-start(f32[4,16,1,128]{3,1,0,2:T(8,128)S(1)} %get-tuple-element.106), channel_id=1, source_target_pairs={{0,4},{4,8},{8,12},{12,16},{16,20},{20,24},{24,28},{1,5},{5,9},{9,... | collective-permute-start | bytes 98312 | tf_op jit(solution)/shard_map/ppermute | solution.py:25
  121.9 1.3 collective-permute-start.13
  123.2 3.9 %collective-permute-done.13 = f32[4,16,1,128]{3,1,0,2:T(8,128)S(1)} collective-permute-done((f32[4,16,1,128]{3,1,0,2:T(8,128)S(1)}, f32[4,16,1,128]{3,1,0,2:T(8,128)S(1)}, u32[]{:S(2)}, u32[]{:S(2)}) %collective-permute-start.13) | collective-permute-done | bytes 32800 | tf_op jit(solution)/shard_map/ppermute | solution.py:26
  127.1 0.2 pad_maximum_fusion.5
  127.4 2.8 %fusion.19 = (f32[4,16,66,1]{3,1,0,2:T(8,128)}, f32[4,16,66,1]{3,1,0,2:T(8,128)}) fusion(f32[4,16,66,128]{3,1,0,2:T(8,128)S(1)} %pad_maximum_fusion.5), kind=kLoop, calls=%fused_computation.61 | loop fusion | bytes 67584 | tf_op jit(solution)/shard_map/slice | solution.py:23
  130.2 2.8 %copy.80 = f32[4,16,66,1]{2,1,3,0:T(8,128)S(1)} copy(f32[4,16,66,1]{3,1,0,2:T(8,128)} %get-tuple-element.96) | data formatting | bytes 33792 | tf_op jit(solution)/shard_map/slice | solution.py:23
  132.9 0.2 collective-permute-start.14
  133.2 2.8 %copy.81 = f32[4,16,66,1]{2,1,3,0:T(8,128)S(1)} copy(f32[4,16,66,1]{3,1,0,2:T(8,128)} %get-tuple-element.97) | data formatting | bytes 33792 | tf_op jit(solution)/shard_map/slice | solution.py:24
  136.0 3.8 %collective-permute-start.15 = (f32[4,16,66,1]{2,1,3,0:T(8,128)S(1)}, f32[4,16,66,1]{2,1,3,0:T(8,128)S(1)}, u32[]{:S(2)}, u32[]{:S(2)}) collective-permute-start(f32[4,16,66,1]{2,1,3,0:T(8,128)S(1)} %copy.81), channel_id=1, source_target_pairs={{1,0},{2,1},{3,2},{0,3},{5,4},{6,5},{7,6},{4,7},{9,8},{10,9},{11,1... | collective-permute-start | bytes 50696 | tf_op jit(solution)/shard_map/ppermute | solution.py:26
  139.8 3.1 %copy.82 = f32[4,16,66,1]{3,1,0,2:T(8,128)} copy(f32[4,16,66,1]{2,1,3,0:T(8,128)S(1)} %collective-permute-done.14) | data formatting | bytes 33792 | tf_op jit(solution)/shard_map/ppermute | solution.py:25
  142.8 3.1 %copy.83 = f32[4,16,66,1]{3,1,0,2:T(8,128)} copy(f32[4,16,66,1]{2,1,3,0:T(8,128)S(1)} %collective-permute-done.15) | data formatting | bytes 33792 | tf_op jit(solution)/shard_map/ppermute | solution.py:26
  145.9 4.0 %pad_maximum_fusion.2 = f32[4,16,66,130]{3,1,0,2:T(8,128)S(1)} fusion(f32[4,16,66,1]{3,1,0,2:T(8,128)} %copy.83, f32[4,16,1,128]{3,1,0,2:T(8,128)S(1)} %collective-permute-done.13, f32[4,16,64,128]{3,1,0,2:T(8,128)S(1)} %fusion.3, f32[4,16,1,128]{3,1,0,2:T(8,128)S(1)} %collective-permute-done.12, f32[4,16,66,1]{3,1,0,2:T(8,128)} %copy.82), kind=kLoop, calls=%fused_computation.2 | loop fusion | flops 2196480 | bytes 4392960 | tf_op jit(solution)/shard_map/concatenate | solution.py:27
  149.9 2.0 %copy-done.1 = f32[4,16,66,130]{3,1,0,2:T(8,128)} copy-done((f32[4,16,66,130]{3,1,0,2:T(8,128)}, f32[4,16,66,130]{3,1,0,2:T(8,128)S(1)}, u32[]{:S(2)}) %copy-start.1) | copy-done | bytes 2196504
  151.9 4.3 %collective-permute-done.16 = f32[4,16,130]{2,1,0:T(8,128)S(1)} collective-permute-done((f32[4,16,130]{2,1,0:T(8,128)S(1)}, f32[4,16,130]{2,1,0:T(8,128)S(1)}, u32[]{:S(2)}, u32[]{:S(2)}) %collective-permute-start.16) | collective-permute-done | bytes 33312 | tf_op jit(solution)/shard_map/ppermute | solution.py:15
  156.2 1.4 collective-permute-start.17
  157.6 5.5 %collective-permute-done.17 = f32[4,16,130]{2,1,0:T(8,128)S(1)} collective-permute-done((f32[4,16,130]{2,1,0:T(8,128)S(1)}, f32[4,16,130]{2,1,0:T(8,128)S(1)}, u32[]{:S(2)}, u32[]{:S(2)}) %collective-permute-start.17) | collective-permute-done | bytes 33312 | tf_op jit(solution)/shard_map/ppermute | solution.py:15
  163.3 1.6 fusion.10
  164.8 1.9 %slice_bitcast_fusion.5 = (f32[16,64,128]{2,0,1:T(8,128)S(1)}, f32[1,16,64,128]{3,1,0,2:T(8,128)S(1)}, f32[1,16,64,128]{3,1,0,2:T(8,128)S(1)}, f32[16,64,128]{2,0,1:T(8,128)S(1)}) fusion(f32[4,16,66,130]{3,1,0,2:T(8,128)} %fusion.10, f32[64,128]{1,0:T(8,128)S(1)} %neg.15, f32[64,128]{1,0:T(8,128)S(1)} %copy-done.3), kind=kLoop, calls=%fused_computation.30 | loop fusion | flops 262144 | bytes 3211264 | tf_op jit(solution)/shard_map/mul | solution.py:45
  166.7 8.6 %fusion.5 = f32[4,16,64,128]{3,1,0,2:T(8,128)S(1)} fusion(f32[1,16,64,128]{3,1,0,2:T(8,128)S(1)} %get-tuple-element.85, f32[1,16,64,128]{3,1,0,2:T(8,128)S(1)} %get-tuple-element.86, f32[4,16,66,130]{3,1,0,2:T(8,128)} %fusion.10, f32[4]{0:T(128)S(1)} %pad.40.clone, f32[16,64,128]{2,0,1:T(8,128)S(1)} %get-tuple-element.87, ...), kind=kLoop, calls=%fused_computation.15 | loop fusion | flops 12058624 | bytes 15335696 | tf_op jit(solution)/shard_map/add | solution.py:115
  175.3 0.2 slice_bitcast_fusion
  175.5 1.0 copy.87
  176.4 1.0 copy.86
  177.4 1.0 copy.85
  178.3 1.0 copy.84
  (50 shorter events, 0.7 us)
Async XLA Ops:
  0.6 2.7 %copy-start.4 = (f32[16,64,128]{2,1,0:T(8,128)S(1)}, f32[16,64,128]{2,1,0:T(8,128)}, u32[]{:S(2)}) copy-start(f32[16,64,128]{2,1,0:T(8,128)} %param.26) | copy-start | bytes 1572868
  0.6 2.7 %copy-start.5 = (f32[16,64,128]{2,1,0:T(8,128)S(1)}, f32[16,64,128]{2,1,0:T(8,128)}, u32[]{:S(2)}) copy-start(f32[16,64,128]{2,1,0:T(8,128)} %param.25) | copy-start | bytes 1572868
  4.2 3.7 %collective-permute-start = (f32[4,16,1,128]{3,1,0,2:T(8,128)S(1)}, f32[4,16,1,128]{3,1,0,2:T(8,128)S(1)}, u32[]{:S(2)}, u32[]{:S(2)}) collective-permute-start(f32[4,16,1,128]{3,1,0,2:T(8,128)S(1)} %get-tuple-element.110), channel_id=1, source_target_pairs={{0,4},{4,8},{8,12},{12,16},{16,20},{20,24},{24,28},{1,5},{5,9},{9,... | collective-permute-start | bytes 98312 | tf_op jit(solution)/shard_map/ppermute | solution.py:25
  6.6 5.2 %collective-permute-start.1 = (f32[4,16,1,128]{3,1,0,2:T(8,128)S(1)}, f32[4,16,1,128]{3,1,0,2:T(8,128)S(1)}, u32[]{:S(2)}, u32[]{:S(2)}) collective-permute-start(f32[4,16,1,128]{3,1,0,2:T(8,128)S(1)} %get-tuple-element.111), channel_id=1, source_target_pairs={{4,0},{8,4},{12,8},{16,12},{20,16},{24,20},{28,24},{5,1},{9,5},{13... | collective-permute-start | bytes 98312 | tf_op jit(solution)/shard_map/ppermute | solution.py:26
  14.9 9.2 %copy-start.6 = (s32[64,128]{1,0:T(8,128)S(1)}, s32[64,128]{1,0:T(8,128)}, u32[]{:S(2)}) copy-start(s32[64,128]{1,0:T(8,128)} %param.27) | copy-start | bytes 98308
  20.4 12.4 %collective-permute-start.3 = (f32[4,16,66,1]{2,1,3,0:T(8,128)S(1)}, f32[4,16,66,1]{2,1,3,0:T(8,128)S(1)}, u32[]{:S(2)}, u32[]{:S(2)}) collective-permute-start(f32[4,16,66,1]{2,1,3,0:T(8,128)S(1)} %copy.73), channel_id=1, source_target_pairs={{1,0},{2,1},{3,2},{0,3},{5,4},{6,5},{7,6},{4,7},{9,8},{10,9},{11,1... | collective-permute-start | bytes 50696 | tf_op jit(solution)/shard_map/ppermute | solution.py:26
  24.0 5.7 %collective-permute-start.2 = (f32[4,16,66,1]{2,1,3,0:T(8,128)S(1)}, f32[4,16,66,1]{2,1,3,0:T(8,128)S(1)}, u32[]{:S(2)}, u32[]{:S(2)}) collective-permute-start(f32[4,16,66,1]{2,1,3,0:T(8,128)S(1)} %copy.72), channel_id=1, source_target_pairs={{0,1},{1,2},{2,3},{3,0},{4,5},{5,6},{6,7},{7,4},{8,9},{9,10},{10,1... | collective-permute-start | bytes 50696 | tf_op jit(solution)/shard_map/ppermute | solution.py:25
  35.9 6.1 %copy-start.7 = (f32[64,128]{1,0:T(8,128)S(1)}, f32[64,128]{1,0:T(8,128)}, u32[]{:S(2)}) copy-start(f32[64,128]{1,0:T(8,128)} %param.29) | copy-start | bytes 98308
  35.9 6.1 %copy-start.8 = (f32[64,128]{1,0:T(8,128)S(1)}, f32[64,128]{1,0:T(8,128)}, u32[]{:S(2)}) copy-start(f32[64,128]{1,0:T(8,128)} %param.28) | copy-start | bytes 98308
  35.9 10.8 %copy-start.10 = (f32[16]{0:T(128)S(1)}, f32[16]{0:T(128)}, u32[]{:S(2)}) copy-start(f32[16]{0:T(128)} %param.32) | copy-start | bytes 196
  35.9 10.8 %copy-start.11 = (f32[16]{0:T(128)S(1)}, f32[16]{0:T(128)}, u32[]{:S(2)}) copy-start(f32[16]{0:T(128)} %param.31) | copy-start | bytes 196
  35.9 10.9 %copy-start.3 = (f32[64,128]{1,0:T(8,128)S(1)}, f32[64,128]{1,0:T(8,128)}, u32[]{:S(2)}) copy-start(f32[64,128]{1,0:T(8,128)} %param.30) | copy-start | bytes 98308
  35.9 16.8 %copy-start.9 = (f32[4]{0:T(128)S(1)}, f32[4]{0:T(128)}, u32[]{:S(2)}) copy-start(f32[4]{0:T(128)} %constant.161.clone) | copy-start | bytes 52
  40.0 2.0 %copy-start = (f32[4,16,66,130]{3,1,0,2:T(8,128)}, f32[4,16,66,130]{3,1,0,2:T(8,128)S(1)}, u32[]{:S(2)}) copy-start(f32[4,16,66,130]{3,1,0,2:T(8,128)S(1)} %pad_maximum_fusion) | copy-start | bytes 6589444
  42.0 4.7 %collective-permute-start.4 = (f32[4,16,130]{2,1,0:T(8,128)S(1)}, f32[4,16,130]{2,1,0:T(8,128)S(1)}, u32[]{:S(2)}, u32[]{:S(2)}) collective-permute-start(f32[4,16,130]{2,1,0:T(8,128)S(1)} %slice_bitcast_fusion.15), channel_id=1, source_target_pairs={{0,1},{1,0},{2,3},{3,2},{4,5},{5,4},{6,7},{7,6},{8,9},{9,8},{10,11... | collective-permute-start | bytes 99848 | tf_op jit(solution)/shard_map/ppermute | solution.py:15
  46.7 5.8 %collective-permute-start.5 = (f32[4,16,130]{2,1,0:T(8,128)S(1)}, f32[4,16,130]{2,1,0:T(8,128)S(1)}, u32[]{:S(2)}, u32[]{:S(2)}) collective-permute-start(f32[4,16,130]{2,1,0:T(8,128)S(1)} %collective-permute-done.4), channel_id=1, source_target_pairs={{0,2},{1,3},{2,0},{3,1},{4,6},{5,7},{6,4},{7,5},{8,10},{9,11},{10,... | collective-permute-start | bytes 99848 | tf_op jit(solution)/shard_map/ppermute | solution.py:15
  64.7 3.4 %collective-permute-start.6 = (f32[4,16,1,128]{3,1,0,2:T(8,128)S(1)}, f32[4,16,1,128]{3,1,0,2:T(8,128)S(1)}, u32[]{:S(2)}, u32[]{:S(2)}) collective-permute-start(f32[4,16,1,128]{3,1,0,2:T(8,128)S(1)} %get-tuple-element.108), channel_id=1, source_target_pairs={{0,4},{4,8},{8,12},{12,16},{16,20},{20,24},{24,28},{1,5},{5,9},{9,... | collective-permute-start | bytes 98312 | tf_op jit(solution)/shard_map/ppermute | solution.py:25
  66.7 5.3 %collective-permute-start.7 = (f32[4,16,1,128]{3,1,0,2:T(8,128)S(1)}, f32[4,16,1,128]{3,1,0,2:T(8,128)S(1)}, u32[]{:S(2)}, u32[]{:S(2)}) collective-permute-start(f32[4,16,1,128]{3,1,0,2:T(8,128)S(1)} %get-tuple-element.109), channel_id=1, source_target_pairs={{4,0},{8,4},{12,8},{16,12},{20,16},{24,20},{28,24},{5,1},{9,5},{13... | collective-permute-start | bytes 98312 | tf_op jit(solution)/shard_map/ppermute | solution.py:26
  77.7 6.6 %collective-permute-start.8 = (f32[4,16,66,1]{2,1,3,0:T(8,128)S(1)}, f32[4,16,66,1]{2,1,3,0:T(8,128)S(1)}, u32[]{:S(2)}, u32[]{:S(2)}) collective-permute-start(f32[4,16,66,1]{2,1,3,0:T(8,128)S(1)} %copy.76), channel_id=1, source_target_pairs={{0,1},{1,2},{2,3},{3,0},{4,5},{5,6},{6,7},{7,4},{8,9},{9,10},{10,1... | collective-permute-start | bytes 50696 | tf_op jit(solution)/shard_map/ppermute | solution.py:25
  80.6 6.9 %collective-permute-start.9 = (f32[4,16,66,1]{2,1,3,0:T(8,128)S(1)}, f32[4,16,66,1]{2,1,3,0:T(8,128)S(1)}, u32[]{:S(2)}, u32[]{:S(2)}) collective-permute-start(f32[4,16,66,1]{2,1,3,0:T(8,128)S(1)} %copy.77), channel_id=1, source_target_pairs={{1,0},{2,1},{3,2},{0,3},{5,4},{6,5},{7,6},{4,7},{9,8},{10,9},{11,1... | collective-permute-start | bytes 50696 | tf_op jit(solution)/shard_map/ppermute | solution.py:26
  94.5 2.0 %copy-start.2 = (f32[4,16,66,130]{3,1,0,2:T(8,128)}, f32[4,16,66,130]{3,1,0,2:T(8,128)S(1)}, u32[]{:S(2)}) copy-start(f32[4,16,66,130]{3,1,0,2:T(8,128)S(1)} %pad_maximum_fusion.1) | copy-start | bytes 6589444
  96.5 4.3 %collective-permute-start.10 = (f32[4,16,130]{2,1,0:T(8,128)S(1)}, f32[4,16,130]{2,1,0:T(8,128)S(1)}, u32[]{:S(2)}, u32[]{:S(2)}) collective-permute-start(f32[4,16,130]{2,1,0:T(8,128)S(1)} %slice_bitcast_fusion.13), channel_id=1, source_target_pairs={{0,1},{1,0},{2,3},{3,2},{4,5},{5,4},{6,7},{7,6},{8,9},{9,8},{10,11... | collective-permute-start | bytes 99848 | tf_op jit(solution)/shard_map/ppermute | solution.py:15
  100.8 6.9 %collective-permute-start.11 = (f32[4,16,130]{2,1,0:T(8,128)S(1)}, f32[4,16,130]{2,1,0:T(8,128)S(1)}, u32[]{:S(2)}, u32[]{:S(2)}) collective-permute-start(f32[4,16,130]{2,1,0:T(8,128)S(1)} %collective-permute-done.10), channel_id=1, source_target_pairs={{0,2},{1,3},{2,0},{3,1},{4,6},{5,7},{6,4},{7,5},{8,10},{9,11},{10,... | collective-permute-start | bytes 99848 | tf_op jit(solution)/shard_map/ppermute | solution.py:15
  119.9 3.3 %collective-permute-start.12 = (f32[4,16,1,128]{3,1,0,2:T(8,128)S(1)}, f32[4,16,1,128]{3,1,0,2:T(8,128)S(1)}, u32[]{:S(2)}, u32[]{:S(2)}) collective-permute-start(f32[4,16,1,128]{3,1,0,2:T(8,128)S(1)} %get-tuple-element.106), channel_id=1, source_target_pairs={{0,4},{4,8},{8,12},{12,16},{16,20},{20,24},{24,28},{1,5},{5,9},{9,... | collective-permute-start | bytes 98312 | tf_op jit(solution)/shard_map/ppermute | solution.py:25
  121.9 5.2 %collective-permute-start.13 = (f32[4,16,1,128]{3,1,0,2:T(8,128)S(1)}, f32[4,16,1,128]{3,1,0,2:T(8,128)S(1)}, u32[]{:S(2)}, u32[]{:S(2)}) collective-permute-start(f32[4,16,1,128]{3,1,0,2:T(8,128)S(1)} %get-tuple-element.107), channel_id=1, source_target_pairs={{4,0},{8,4},{12,8},{16,12},{20,16},{24,20},{28,24},{5,1},{9,5},{13... | collective-permute-start | bytes 98312 | tf_op jit(solution)/shard_map/ppermute | solution.py:26
  132.9 6.8 %collective-permute-start.14 = (f32[4,16,66,1]{2,1,3,0:T(8,128)S(1)}, f32[4,16,66,1]{2,1,3,0:T(8,128)S(1)}, u32[]{:S(2)}, u32[]{:S(2)}) collective-permute-start(f32[4,16,66,1]{2,1,3,0:T(8,128)S(1)} %copy.80), channel_id=1, source_target_pairs={{0,1},{1,2},{2,3},{3,0},{4,5},{5,6},{6,7},{7,4},{8,9},{9,10},{10,1... | collective-permute-start | bytes 50696 | tf_op jit(solution)/shard_map/ppermute | solution.py:25
  136.0 6.9 %collective-permute-start.15 = (f32[4,16,66,1]{2,1,3,0:T(8,128)S(1)}, f32[4,16,66,1]{2,1,3,0:T(8,128)S(1)}, u32[]{:S(2)}, u32[]{:S(2)}) collective-permute-start(f32[4,16,66,1]{2,1,3,0:T(8,128)S(1)} %copy.81), channel_id=1, source_target_pairs={{1,0},{2,1},{3,2},{0,3},{5,4},{6,5},{7,6},{4,7},{9,8},{10,9},{11,1... | collective-permute-start | bytes 50696 | tf_op jit(solution)/shard_map/ppermute | solution.py:26
  149.9 2.0 %copy-start.1 = (f32[4,16,66,130]{3,1,0,2:T(8,128)}, f32[4,16,66,130]{3,1,0,2:T(8,128)S(1)}, u32[]{:S(2)}) copy-start(f32[4,16,66,130]{3,1,0,2:T(8,128)S(1)} %pad_maximum_fusion.2) | copy-start | bytes 6589444
  151.9 4.3 %collective-permute-start.16 = (f32[4,16,130]{2,1,0:T(8,128)S(1)}, f32[4,16,130]{2,1,0:T(8,128)S(1)}, u32[]{:S(2)}, u32[]{:S(2)}) collective-permute-start(f32[4,16,130]{2,1,0:T(8,128)S(1)} %slice_bitcast_fusion.11), channel_id=1, source_target_pairs={{0,1},{1,0},{2,3},{3,2},{4,5},{5,4},{6,7},{7,6},{8,9},{9,8},{10,11... | collective-permute-start | bytes 99848 | tf_op jit(solution)/shard_map/ppermute | solution.py:15
  156.2 6.9 %collective-permute-start.17 = (f32[4,16,130]{2,1,0:T(8,128)S(1)}, f32[4,16,130]{2,1,0:T(8,128)S(1)}, u32[]{:S(2)}, u32[]{:S(2)}) collective-permute-start(f32[4,16,130]{2,1,0:T(8,128)S(1)} %collective-permute-done.16), channel_id=1, source_target_pairs={{0,2},{1,3},{2,0},{3,1},{4,6},{5,7},{6,4},{7,5},{8,10},{9,11},{10,... | collective-permute-start | bytes 99848 | tf_op jit(solution)/shard_map/ppermute | solution.py:15
where the time goes:
time: 180 us; the launch traced here: 179 us
  local copies, waits for them, and re-layouts  56.4 us (31%)
  other arithmetic  50 us (28%)
  waiting for transfers between devices  47.1 us (26%)
  starting transfers between devices  24.8 us (14%)
    ppermute x6, waiting for transfers between devices, partner(): return lax.ppermute(value, axis, pairs)  29.9 us
    add x3, other arithmetic, on_device(): updated = middle + time_step * local_mask[None] * change  25.7 us
    slice x9, local copies, waits for them, and re-layouts, with_halo(): last = lax.slice_in_dim(value, length - width, length, axis=dim)  16.8 us
    ppermute x6, starting transfers between devices, with_halo(): after = lax.ppermute(initial, axis, down)  15.3 us
    concatenate x6, other arithmetic, with_halo(): value = jnp.concatenate([before, value, after], axis=dim)  12.8 us
    ppermute x6, waiting for transfers between devices, with_halo(): after = lax.ppermute(initial, axis, down)  11.5 us
    unnamed x31, local copies, waits for them, and re-layouts  10.3 us
    ppermute x3, local copies, waits for them, and re-layouts, with_halo(): after = lax.ppermute(initial, axis, down)  9.22 us
  transfers between devices with their start and end apart: 18, of which 10 were waited for; matrix products, arithmetic and copies ran while one was open for 8% of the time, Pallas kernels for 0%

commit v1 on v0

v1 whole, which is shorter than its diff:
```python
import functools

import jax
import jax.numpy as jnp
from jax import lax
from jax.experimental import pallas as pl
from jax.experimental.pallas import tpu as pltpu
from jax.sharding import PartitionSpec as P

STEPS = 3
RIM = 3
time_step = 0.2

MESH = pl.DeviceIdType.MESH


def lanes(shape):
    return lax.broadcasted_iota(jnp.int32, shape, len(shape) - 1)


def exchange(
    x0, x1, x2, x3, bathy, wide, high, vort,
    rows_n, rows_s, strips, strip_n, strip_s,
    out_n, out_s, packed, to_side, from_side, edge_n, edge_s,
    send_sem, recv_sem,
):
    fields = (x0, x1, x2, x3)
    levels, height, width = x0.shape
    lat, lon = lax.axis_index("lat"), lax.axis_index("lon")
    lats, lons = lax.axis_size("lat"), lax.axis_size("lon")
    last = lat == lats - 1
    east = (lat, lax.rem(lon + 1, lons))
    west = (lat, lax.rem(lon + lons - 1, lons))
    north = (
        jnp.where(last, lat, lat + 1),
        jnp.where(last, lons - 1 - lon, lon),
    )
    south = (lat - 1, lon)

    barrier = pltpu.get_barrier_semaphore()
    for peer in (east, west, north):
        pl.semaphore_signal(barrier, inc=1, device_id=peer, device_id_type=MESH)

    @pl.when(lat > 0)
    def _():
        pl.semaphore_signal(barrier, inc=1, device_id=south, device_id_type=MESH)

    lane = lanes((8, width))
    group = lane // 8
    within = lane - group * 8

    @pl.loop(0, height // 8)
    def _(tile):
        rows = pl.ds(pl.multiple_of(tile * 8, 8), 8)
        cols = []
        for f in range(4):
            acc = pltpu.roll(fields[f][0, rows, :], RIM, 1)
            for level in range(1, levels):
                moved = pltpu.roll(fields[f][level, rows, :], (8 * level + RIM) % width, 1)
                acc = jnp.where(group == level, moved, acc)
            packed[f, rows, :] = acc
            cols.append(acc)
        acc = jnp.zeros((8, width), jnp.float32)
        metrics = (bathy[rows, :].astype(jnp.float32), wide[rows, :], high[rows, :], vort[rows, :])
        for m in range(4):
            acc = jnp.where(group == m, pltpu.roll(metrics[m], 8 * m + RIM, 1), acc)
        packed[4, rows, :] = acc
        for pair in range(2):
            one, two = cols[2 * pair], cols[2 * pair + 1]
            to_side[0, pair, rows, :] = jnp.where(within < 4, one, pltpu.roll(two, 4, 1))
            to_side[1, pair, rows, :] = jnp.where(within < 3, pltpu.roll(two, width - 3, 1), one)
        to_side[0, 2, rows, :] = acc
        to_side[1, 2, rows, :] = acc

    @pl.when(lat > 0)
    def _():
        pl.semaphore_wait(barrier, 4)

    @pl.when(lat == 0)
    def _():
        pl.semaphore_wait(barrier, 3)

    def remote(src, dst, which, arrive, peer):
        return pltpu.make_async_remote_copy(
            src_ref=src, dst_ref=dst, send_sem=send_sem.at[which], recv_sem=recv_sem.at[arrive],
            device_id=peer, device_id_type=MESH,
        )

    go_east = remote(to_side.at[0], from_side.at[0], 0, 0, east)
    go_west = remote(to_side.at[1], from_side.at[1], 1, 1, west)
    go_east.start()
    go_west.start()

    for f in range(4):
        for r in range(RIM):
            at = (f * RIM + r) * levels
            out_s[at : at + levels, :] = fields[f][:, r, :]
            out_n[at : at + levels, :] = fields[f][:, height - RIM + r, :]
    base = 4 * RIM * levels
    out_s[base : base + 16, :] = jnp.zeros((16, width), jnp.float32)
    out_n[base : base + 16, :] = jnp.zeros((16, width), jnp.float32)
    for m, metric in enumerate((bathy, wide, high, vort)):
        out_s[base + m * RIM : base + (m + 1) * RIM, :] = metric[0:RIM, :].astype(jnp.float32)
        out_n[base + m * RIM : base + (m + 1) * RIM, :] = metric[height - RIM :, :].astype(jnp.float32)

    def rows_out(to_n, to_s, recv_n, recv_s, first):
        up = remote(to_n, recv_s, first, first, north)
        fold = remote(to_n, recv_n, first, first + 1, north)
        down = remote(to_s, recv_n, first + 1, first + 1, south)

        @pl.when(last)
        def _():
            fold.start()

        @pl.when(lat < lats - 1)
        def _():
            up.start()

        @pl.when(lat > 0)
        def _():
            down.start()

        return up, down

    def rows_in(up, down):
        down.wait_recv()

        @pl.when(lat > 0)
        def _():
            up.wait_recv()

    def rows_sent(up, down):
        up.wait_send()

        @pl.when(lat > 0)
        def _():
            down.wait_send()

    @pl.when(lat == 0)
    def _():
        rows_s[...] = jnp.zeros(rows_s.shape, jnp.float32)
        strip_s[...] = jnp.zeros(strip_s.shape, jnp.float32)

    main = rows_out(out_n, out_s, rows_n, rows_s, 2)

    go_east.wait_recv()
    go_west.wait_recv()

    @pl.loop(0, height // 8)
    def _(tile):
        rows = pl.ds(pl.multiple_of(tile * 8, 8), 8)
        for f in range(5):
            own = packed[f, rows, :]
            got_w = from_side[0, f // 2, rows, :]
            got_e = from_side[1, f // 2, rows, :]
            if f % 2 == 1:
                got_w = pltpu.roll(got_w, width - 4, 1)
                got_e = pltpu.roll(got_e, 3, 1)
            strips[0, f, rows, :] = jnp.where(within < RIM, got_w, own)
            strips[1, f, rows, :] = jnp.where(within < RIM, own, got_e)

    edge_n[30:32, :] = jnp.zeros((2, width), jnp.float32)
    edge_s[30:32, :] = jnp.zeros((2, width), jnp.float32)
    for side in range(2):
        for f in range(5):
            at = (side * 5 + f) * RIM
            edge_s[at : at + RIM, :] = strips[side, f, 0:RIM, :]
            edge_n[at : at + RIM, :] = strips[side, f, height - RIM : height, :]
    ends = rows_out(edge_n, edge_s, strip_n, strip_s, 4)

    go_east.wait_send()
    go_west.wait_send()
    rows_in(*main)
    rows_in(*ends)
    rows_sent(*main)
    rows_sent(*ends)


def substeps(
    tracer_mix, momentum_mix, x0, x1, x2, x3, bathy, wide, high, vort,
    rows_n, rows_s, strips, strip_n, strip_s,
    y0, y1, y2, y3,
    first, second, metric, sides, sides_next, side_metric, link,
):
    fields = (x0, x1, x2, x3)
    outs = (y0, y1, y2, y3)
    levels, height, width = x0.shape
    deep = height + 8
    tiles = deep // 8
    lat = lax.axis_index("lat")
    lats = lax.axis_size("lat")
    last, bottom = lat == lats - 1, lat == 0
    signs = (1.0, 1.0, -1.0, -1.0)
    lane = lanes((8, width))
    row = lax.broadcasted_iota(jnp.int32, (8, width), 0)
    group = lane // 8
    within = lane - group * 8

    def mirrored(value, index):
        pieces = [
            jnp.take_along_axis(value[i : i + 8, :], index, axis=1)
            for i in range(0, value.shape[0], 8)
        ]
        return jnp.concatenate(pieces, axis=0)

    far = rows_n[...]
    flipped = mirrored(far, width - 1 - lane)
    near = rows_s[...]
    side_far = strip_n[...]
    side_flipped = mirrored(side_far, group * 8 + jnp.where(within < 6, 5 - within, within))
    side_near = strip_s[...]

    safe = (0.0, 1.0, 1.0, 0.0)
    base = 4 * RIM * levels
    for m, value in enumerate((bathy, wide, high, vort)):
        metric[m, 0:height, :] = value[...].astype(jnp.float32)
        metric[m, height:deep, :] = jnp.full((8, width), safe[m], jnp.float32)
        for r in range(RIM):
            at = base + m * RIM + r
            fold = base + m * RIM + RIM - 1 - r
            metric[m, height + r : height + r + 1, :] = jnp.where(
                last, flipped[fold : fold + 1, :], far[at : at + 1, :]
            )
            metric[m, deep - RIM + r : deep - RIM + r + 1, :] = jnp.where(
                bottom, safe[m], near[at : at + 1, :]
            )

    for f in range(4):
        for r in range(RIM):
            at = (f * RIM + r) * levels
            fold = (f * RIM + RIM - 1 - r) * levels
            first[f, :, height + r, :] = jnp.where(
                last, signs[f] * flipped[fold : fold + levels, :], far[at : at + levels, :]
            )
            first[f, :, deep - RIM + r, :] = near[at : at + levels, :]

    for side in range(2):
        for f in range(5):
            sides[side, f, 0:height, :] = strips[side, f, :, :]
            if f == 4:
                fill = jnp.where((group == 1) | (group == 2), 1.0, 0.0)
            else:
                fill = jnp.zeros((8, width), jnp.float32)
            sides[side, f, height:deep, :] = fill
            for r in range(RIM):
                at = (side * 5 + f) * RIM + r
                fold = ((1 - side) * 5 + f) * RIM + RIM - 1 - r
                sign = 1.0 if f == 4 else signs[f]
                sides[side, f, height + r : height + r + 1, :] = jnp.where(
                    last, sign * side_flipped[fold : fold + 1, :], side_far[at : at + 1, :]
                )
                got = side_near[at : at + 1, :]
                if f == 4:
                    got = jnp.where(bottom, fill[0:1, :], got)
                sides[side, f, deep - RIM + r : deep - RIM + r + 1, :] = got

    def factors(bath, we, sn, vo):
        a, b = 1.0 / we, 1.0 / sn
        return (
            bath, time_step * a * a, time_step * b * b,
            0.5 * time_step * a, 0.5 * time_step * b, time_step * vo,
        )

    @pl.loop(0, tiles)
    def _(tile):
        rows = pl.ds(pl.multiple_of(tile * 8, 8), 8)
        made = factors(*[metric[m, rows, :] for m in range(4)])
        for m in range(6):
            metric[m, rows, :] = made[m]
        for side in range(2):
            mixed = sides[side, 4, rows, :]
            spread = []
            for m in range(4):
                value = jnp.where(group == m, mixed, 0.0)
                for hop in (8, 16, 32, 64):
                    value = value + pltpu.roll(value, hop, 1)
                spread.append(value)
            made = factors(*spread)
            for m in range(6):
                side_metric[side, m, rows, :] = made[m]
            wet = made[0] > group.astype(jnp.float32)
            for f in range(4):
                sides[side, f, rows, :] = jnp.where(wet, sides[side, f, rows, :], 0.0)

    @pl.loop(0, levels)
    def _(level):
        number = level.astype(jnp.float32)
        for t in range(tiles):
            rows = slice(8 * t, 8 * t + 8)
            wet = metric[0, rows, :] > number
            for f in range(4):
                if t < tiles - 1:
                    value = fields[f][level, rows, :]
                else:
                    value = first[f, level, rows, :]
                    value = jnp.where((row < RIM) | (row >= 8 - RIM), value, 0.0)
                first[f, level, rows, :] = jnp.where(wet, value, 0.0)

    mix_t = jnp.zeros((8, width), jnp.float32)
    mix_m = jnp.zeros((8, width), jnp.float32)
    for level in range(levels):
        mix_t = jnp.where(group == level, tracer_mix[level], mix_t)
        mix_m = jnp.where(group == level, momentum_mix[level], mix_m)

    def advance(read, seam, table, number, mixes, t):
        centre = [read(f, 8 * t, 8) for f in range(4)]

        def north_of(f):
            if t < tiles - 1:
                return read(f, 8 * t + 1, 8)
            wrapped = pltpu.roll(read(f, 0, 8), 7, 0)
            return jnp.where(row == 7, wrapped, pltpu.roll(centre[f], 7, 0))

        def south_of(f):
            if t > 0:
                return read(f, 8 * t - 1, 8)
            wrapped = pltpu.roll(read(f, deep - 8, 8), 1, 0)
            return jnp.where(row == 0, wrapped, pltpu.roll(centre[f], 1, 0))

        bath, a2, b2, ah, bh, vo = [table(m, 8 * t) for m in range(6)]
        wet = bath > number
        a2 = jnp.where(wet, a2, 0.0)
        b2 = jnp.where(wet, b2, 0.0)
        u, v = centre[2], centre[3]
        du, dv = u * ah, v * bh
        results = []
        for f in range(4):
            if f % 2 == 0:
                da, db = mixes[f // 2] * a2, mixes[f // 2] * b2
                ce, cw, cn, cs = da - du, da + du, db - dv, db + dv
                cc = 1.0 - 2.0 * (da + db)
            c = centre[f]
            if seam is None:
                e, w = pltpu.roll(c, width - 1, 1), pltpu.roll(c, 1, 1)
            else:
                z = seam(f, t)
                e = pltpu.roll(jnp.where(lane == 0, z, c), width - 1, 1)
                w = pltpu.roll(jnp.where(lane == width - 1, z, c), 1, 1)
            new = cc * c + (ce * e + cw * w) + (cn * north_of(f) + cs * south_of(f))
            if f == 2:
                new = new + vo * v
            if f == 3:
                new = new - vo * u
            results.append(new)
        return results

    def main_step(source, store, count):
        @pl.loop(0, levels)
        def _(level):
            number = level.astype(jnp.float32)
            mixes = (tracer_mix[level], momentum_mix[level])
            for t in range(count):
                new = advance(
                    lambda f, start, size: source[f, level, start : start + size, :],
                    lambda f, t: pltpu.roll(link[f, 8 * t : 8 * t + 8, :], width - 3 - 8 * level, 1),
                    lambda m, start: metric[m, start : start + 8, :],
                    number, mixes, t,
                )
                for f in range(4):
                    store(f, level, t, new[f])

    def side_step(source, target):
        for side in range(2):
            for t in range(tiles):
                new = advance(
                    lambda f, start, size: source[side, f, start : start + size, :],
                    None,
                    lambda m, start: side_metric[side, m, start : start + 8, :],
                    group.astype(jnp.float32), (mix_t, mix_m), t,
                )
                for f in range(4):
                    target[side, f, 8 * t : 8 * t + 8, :] = new[f]

    def join(source):
        for f in range(4):
            for t in range(tiles):
                rows = slice(8 * t, 8 * t + 8)
                link[f, rows, :] = jnp.where(within == 2, source[0, f, rows, :], source[1, f, rows, :])

    def into(buffer):
        def store(f, level, t, value):
            buffer[f, level, 8 * t : 8 * t + 8, :] = value
        return store

    def final(f, level, t, value):
        outs[f][level, 8 * t : 8 * t + 8, :] = value

    state, spare = first, second
    side_state, side_spare = sides, sides_next
    for step in range(STEPS):
        join(side_state)
        if step < STEPS - 1:
            main_step(state, into(spare), tiles)
            side_step(side_state, side_spare)
        else:
            main_step(state, final, tiles - 1)
        state, spare = spare, state
        side_state, side_spare = side_spare, side_state


def on_device(
    potential_heat_state,
    saltiness_anomaly,
    first_current_component,
    second_current_component,
    bathymetry_layer_total,
    westeast_cell_extent,
    southnorth_cell_extent,
    planetary_vorticity,
    scalar_mixing_factor,
    momentum_mixing_factor,
):
    fields = (potential_heat_state, saltiness_anomaly, first_current_component, second_current_component)
    metrics = (bathymetry_layer_total, westeast_cell_extent, southnorth_cell_extent, planetary_vorticity)
    levels, height, width = potential_heat_state.shape
    f32 = jnp.float32
    message = 4 * RIM * levels + 16
    deep = height + 8
    vmem = pl.BlockSpec(memory_space=pltpu.VMEM)
    smem = pl.BlockSpec(memory_space=pltpu.SMEM)
    rims = pl.pallas_call(
        exchange,
        out_shape=(
            jax.ShapeDtypeStruct((message, width), f32),
            jax.ShapeDtypeStruct((message, width), f32),
            jax.ShapeDtypeStruct((2, 5, height, width), f32),
            jax.ShapeDtypeStruct((32, width), f32),
            jax.ShapeDtypeStruct((32, width), f32),
        ),
        in_specs=[vmem] * 8,
        out_specs=[vmem] * 5,
        scratch_shapes=[
            pltpu.VMEM((message, width), f32),
            pltpu.VMEM((message, width), f32),
            pltpu.VMEM((5, height, width), f32),
            pltpu.VMEM((2, 3, height, width), f32),
            pltpu.VMEM((2, 3, height, width), f32),
            pltpu.VMEM((32, width), f32),
            pltpu.VMEM((32, width), f32),
            pltpu.SemaphoreType.DMA((6,)),
            pltpu.SemaphoreType.DMA((6,)),
        ],
        compiler_params=pltpu.CompilerParams(
            collective_id=0, has_side_effects=True, vmem_limit_bytes=16 * 2**20
        ),
        name="exchange",
    )(*fields, *metrics)
    whole = jax.ShapeDtypeStruct((levels, height, width), f32)
    return pl.pallas_call(
        substeps,
        out_shape=(whole,) * 4,
        in_specs=[smem] * 2 + [vmem] * 13,
        out_specs=[vmem] * 4,
        scratch_shapes=[
            pltpu.VMEM((4, levels, deep, width), f32),
            pltpu.VMEM((4, levels, deep, width), f32),
            pltpu.VMEM((6, deep, width), f32),
            pltpu.VMEM((2, 5, deep, width), f32),
            pltpu.VMEM((2, 5, deep, width), f32),
            pltpu.VMEM((2, 6, deep, width), f32),
            pltpu.VMEM((4, deep, width), f32),
        ],
        compiler_params=pltpu.CompilerParams(vmem_limit_bytes=24 * 2**20),
        name="substeps",
    )(scalar_mixing_factor, momentum_mixing_factor, *fields, *metrics, *rims)


def solution(mesh):
    state, plane = P(None, "lat", "lon"), P("lat", "lon")
    return jax.shard_map(
        on_device,
        mesh=mesh,
        in_specs=(state,) * 4 + (plane,) * 4 + (P(), P()),
        out_specs=(state,) * 4,
        check_vma=False,
    )
```

time: 180 us -> 38.6 us (0.21)
  the two profiles are of different devices: /device:TPU:0 before, /device:TPU:13 now
where the time goes in v1:
time: 38.6 us; the launch traced here: 38 us
  Pallas kernels  29.4 us (76%)
  local copies, waits for them, and re-layouts  7.8 us (20%)
  between operations  0.77 us (2%)
    pallas_call x1, Pallas kernels, on_device(): pl.pallas_call(substeps, out_shape=(whole,) * 4, in_specs=[smem] * 2 + [v...  15.8 us
    pallas_call x1, Pallas kernels, on_device(): pl.pallas_call(exchange, out_shape=(jax.ShapeDtypeStruct((message, width)...  13.6 us
    unnamed x36, local copies, waits for them, and re-layouts  7.8 us

profile of v1, /device:TPU:13, one launch (start us, length us, event | category | flops | bytes accessed | tf_op | source)
XLA Modules:
  0.0 38.0 jit_solution(18389253407195671889)
XLA Ops:
  0.6 0.0 copy-start
  0.6 1.0 %copy-done = f32[16,64,128]{2,1,0:T(8,128)S(1)} copy-done((f32[16,64,128]{2,1,0:T(8,128)S(1)}, f32[16,64,128]{2,1,0:T(8,128)}, u32[]{:S(2)}) %copy-start) | copy-done | bytes 524312
  1.7 0.0 copy-start.2
  1.7 1.0 %copy-done.2 = f32[16,64,128]{2,1,0:T(8,128)S(1)} copy-done((f32[16,64,128]{2,1,0:T(8,128)S(1)}, f32[16,64,128]{2,1,0:T(8,128)}, u32[]{:S(2)}) %copy-start.2) | copy-done | bytes 524312
  2.7 0.0 copy-start.4
  2.7 1.0 %copy-done.4 = f32[16,64,128]{2,1,0:T(8,128)S(1)} copy-done((f32[16,64,128]{2,1,0:T(8,128)S(1)}, f32[16,64,128]{2,1,0:T(8,128)}, u32[]{:S(2)}) %copy-start.4) | copy-done | bytes 524312
  3.8 0.0 copy-start.6
  3.8 1.0 %copy-done.6 = f32[16,64,128]{2,1,0:T(8,128)S(1)} copy-done((f32[16,64,128]{2,1,0:T(8,128)S(1)}, f32[16,64,128]{2,1,0:T(8,128)}, u32[]{:S(2)}) %copy-start.6) | copy-done | bytes 524312
  4.8 0.0 copy-start.8
  4.8 0.8 %copy-done.8 = s32[64,128]{1,0:T(8,128)S(1)} copy-done((s32[64,128]{1,0:T(8,128)S(1)}, s32[64,128]{1,0:T(8,128)}, u32[]{:S(2)}) %copy-start.8) | copy-done | bytes 32792
  5.6 0.0 copy-start.10
  5.6 0.8 %copy-done.10 = f32[64,128]{1,0:T(8,128)S(1)} copy-done((f32[64,128]{1,0:T(8,128)S(1)}, f32[64,128]{1,0:T(8,128)}, u32[]{:S(2)}) %copy-start.10) | copy-done | bytes 32792
  6.3 0.0 copy-start.12
  6.3 0.8 %copy-done.12 = f32[64,128]{1,0:T(8,128)S(1)} copy-done((f32[64,128]{1,0:T(8,128)S(1)}, f32[64,128]{1,0:T(8,128)}, u32[]{:S(2)}) %copy-start.12) | copy-done | bytes 32792
  7.1 0.0 copy-start.14
  7.1 0.8 %copy-done.14 = f32[64,128]{1,0:T(8,128)S(1)} copy-done((f32[64,128]{1,0:T(8,128)S(1)}, f32[64,128]{1,0:T(8,128)}, u32[]{:S(2)}) %copy-start.14) | copy-done | bytes 32792
  7.8 0.0 copy-start.1
  7.8 0.0 copy-start.3
  7.8 0.0 copy-start.5
  7.8 0.0 copy-start.7
  7.8 0.0 copy-start.9
  7.9 0.0 copy-start.11
  7.9 0.0 copy-start.13
  7.9 0.0 copy-start.15
  7.9 13.6 %exchange.1 = (f32[208,128]{1,0:T(8,128)S(1)}, f32[208,128]{1,0:T(8,128)S(1)}, f32[2,5,64,128]{3,2,1,0:T(8,128)S(1)}, f32[32,128]{1,0:T(8,128)S(1)}, f32[32,128]{1,0:T(8,128)S(1)}) custom-call(f32[16,64,128]{2,1,0:T(8,128)S(1)} %copy-done, f32[16,64,128]{2,1,0:T(8,128)S(1)} %copy-done.2, f32[16,64,128]{2,1,0:T(8,128)S(1)} %copy-done.4, ...), custom_call_target="tpu_custom_call" | custom-call | tf_op jit(solution)/shard_map/exchange/pallas_call | solution.py:421
  21.5 0.0 copy-start.16
  21.5 0.0 copy-start.17
  21.5 0.0 copy-done.1
  21.5 0.0 copy-done.3
  21.6 0.0 copy-done.5
  21.6 0.0 copy-done.7
  21.6 0.0 copy-done.9
  21.6 0.0 copy-done.11
  21.6 0.0 copy-done.13
  21.6 0.0 copy-done.15
  21.6 0.6 %copy-done.16 = f32[16]{0:T(128)S(1)} copy-done((f32[16]{0:T(128)S(1)}, f32[16]{0:T(128)}, u32[]{:S(2)}) %copy-start.16) | copy-done | bytes 88
  22.2 0.0 copy-done.17
  22.2 15.8 %substeps.1 = (f32[16,64,128]{2,1,0:T(8,128)}, f32[16,64,128]{2,1,0:T(8,128)}, f32[16,64,128]{2,1,0:T(8,128)}, f32[16,64,128]{2,1,0:T(8,128)}) custom-call(f32[16]{0:T(128)S(1)} %copy-done.16, f32[16]{0:T(128)S(1)} %copy-done.17, f32[16,64,128]{2,1,0:T(8,128)S(1)} %copy-done.1, f32[16,64,128]{2,1,0:T(8,128)S(1)} %copy-done.3, f32[16,64,128]{2,1,0:T(8,128)S(1)} %copy-done.5, ...), custom_call_target="tpu_custom_call" | custom-call | tf_op jit(solution)/shard_map/substeps/pallas_call | solution.py:449
Async XLA Ops:
  0.6 1.0 %copy-start = (f32[16,64,128]{2,1,0:T(8,128)S(1)}, f32[16,64,128]{2,1,0:T(8,128)}, u32[]{:S(2)}) copy-start(f32[16,64,128]{2,1,0:T(8,128)} %x0.3) | copy-start | bytes 1572868
  1.7 1.0 %copy-start.2 = (f32[16,64,128]{2,1,0:T(8,128)S(1)}, f32[16,64,128]{2,1,0:T(8,128)}, u32[]{:S(2)}) copy-start(f32[16,64,128]{2,1,0:T(8,128)} %x1.3) | copy-start | bytes 1572868
  2.7 1.0 %copy-start.4 = (f32[16,64,128]{2,1,0:T(8,128)S(1)}, f32[16,64,128]{2,1,0:T(8,128)}, u32[]{:S(2)}) copy-start(f32[16,64,128]{2,1,0:T(8,128)} %x2.3) | copy-start | bytes 1572868
  3.8 1.0 %copy-start.6 = (f32[16,64,128]{2,1,0:T(8,128)S(1)}, f32[16,64,128]{2,1,0:T(8,128)}, u32[]{:S(2)}) copy-start(f32[16,64,128]{2,1,0:T(8,128)} %x3.3) | copy-start | bytes 1572868
  4.8 0.8 %copy-start.8 = (s32[64,128]{1,0:T(8,128)S(1)}, s32[64,128]{1,0:T(8,128)}, u32[]{:S(2)}) copy-start(s32[64,128]{1,0:T(8,128)} %bathy.3) | copy-start | bytes 98308
  5.6 0.8 %copy-start.10 = (f32[64,128]{1,0:T(8,128)S(1)}, f32[64,128]{1,0:T(8,128)}, u32[]{:S(2)}) copy-start(f32[64,128]{1,0:T(8,128)} %wide.3) | copy-start | bytes 98308
  6.3 0.8 %copy-start.12 = (f32[64,128]{1,0:T(8,128)S(1)}, f32[64,128]{1,0:T(8,128)}, u32[]{:S(2)}) copy-start(f32[64,128]{1,0:T(8,128)} %high.3) | copy-start | bytes 98308
  7.1 0.8 %copy-start.14 = (f32[64,128]{1,0:T(8,128)S(1)}, f32[64,128]{1,0:T(8,128)}, u32[]{:S(2)}) copy-start(f32[64,128]{1,0:T(8,128)} %vort.3) | copy-start | bytes 98308
  7.8 13.7 %copy-start.1 = (f32[16,64,128]{2,1,0:T(8,128)S(1)}, f32[16,64,128]{2,1,0:T(8,128)}, u32[]{:S(2)}) copy-start(f32[16,64,128]{2,1,0:T(8,128)} %x0.3) | copy-start | bytes 1572868
  7.8 13.7 %copy-start.3 = (f32[16,64,128]{2,1,0:T(8,128)S(1)}, f32[16,64,128]{2,1,0:T(8,128)}, u32[]{:S(2)}) copy-start(f32[16,64,128]{2,1,0:T(8,128)} %x1.3) | copy-start | bytes 1572868
  7.8 13.7 %copy-start.5 = (f32[16,64,128]{2,1,0:T(8,128)S(1)}, f32[16,64,128]{2,1,0:T(8,128)}, u32[]{:S(2)}) copy-start(f32[16,64,128]{2,1,0:T(8,128)} %x2.3) | copy-start | bytes 1572868
  7.8 13.7 %copy-start.7 = (f32[16,64,128]{2,1,0:T(8,128)S(1)}, f32[16,64,128]{2,1,0:T(8,128)}, u32[]{:S(2)}) copy-start(f32[16,64,128]{2,1,0:T(8,128)} %x3.3) | copy-start | bytes 1572868
  7.8 13.7 %copy-start.9 = (s32[64,128]{1,0:T(8,128)S(1)}, s32[64,128]{1,0:T(8,128)}, u32[]{:S(2)}) copy-start(s32[64,128]{1,0:T(8,128)} %bathy.3) | copy-start | bytes 98308
  7.9 13.7 %copy-start.11 = (f32[64,128]{1,0:T(8,128)S(1)}, f32[64,128]{1,0:T(8,128)}, u32[]{:S(2)}) copy-start(f32[64,128]{1,0:T(8,128)} %wide.3) | copy-start | bytes 98308
  7.9 13.7 %copy-start.13 = (f32[64,128]{1,0:T(8,128)S(1)}, f32[64,128]{1,0:T(8,128)}, u32[]{:S(2)}) copy-start(f32[64,128]{1,0:T(8,128)} %high.3) | copy-start | bytes 98308
  7.9 13.7 %copy-start.15 = (f32[64,128]{1,0:T(8,128)S(1)}, f32[64,128]{1,0:T(8,128)}, u32[]{:S(2)}) copy-start(f32[64,128]{1,0:T(8,128)} %vort.3) | copy-start | bytes 98308
  21.5 0.7 %copy-start.16 = (f32[16]{0:T(128)S(1)}, f32[16]{0:T(128)}, u32[]{:S(2)}) copy-start(f32[16]{0:T(128)} %tracer_mix.1) | copy-start | bytes 196
  21.5 0.7 %copy-start.17 = (f32[16]{0:T(128)S(1)}, f32[16]{0:T(128)}, u32[]{:S(2)}) copy-start(f32[16]{0:T(128)} %momentum_mix.1) | copy-start | bytes 196

commit v2 on v1

v2 whole, which is shorter than its diff:
```python
import functools

import jax
import jax.numpy as jnp
from jax import lax
from jax.experimental import pallas as pl
from jax.experimental.pallas import tpu as pltpu
from jax.sharding import PartitionSpec as P

STEPS = 3
RIM = 3
time_step = 0.2

MESH = pl.DeviceIdType.MESH


def lanes(shape):
    return lax.broadcasted_iota(jnp.int32, shape, len(shape) - 1)


def factors(bath, we, sn, vo):
    a, b = 1.0 / we, 1.0 / sn
    return (
        bath, time_step * a * a, time_step * b * b,
        0.5 * time_step * a, 0.5 * time_step * b, time_step * vo,
    )


def exchange(
    x0, x1, x2, x3, bathy, wide, high, vort,
    state, table, sides, side_metric,
    field, whole, bath, metric,
    rows_n, rows_s, strips, strip_n, strip_s,
    out_n, out_s, packed, to_side, from_side, edge_n, edge_s,
    send_sem, recv_sem, load_sem,
):
    levels, width = state.shape[2], state.shape[3]
    height = wide.shape[0]
    deep = height + 8
    lat, lon = lax.axis_index("lat"), lax.axis_index("lon")
    lats, lons = lax.axis_size("lat"), lax.axis_size("lon")
    last, bottom = lat == lats - 1, lat == 0
    east = (lat, lax.rem(lon + 1, lons))
    west = (lat, lax.rem(lon + lons - 1, lons))
    north = (
        jnp.where(last, lat, lat + 1),
        jnp.where(last, lons - 1 - lon, lon),
    )
    south = (lat - 1, lon)

    loads = [
        pltpu.make_async_copy(x, field.at[f], load_sem.at[f]) for f, x in enumerate((x0, x1, x2, x3))
    ]
    loads.append(pltpu.make_async_copy(bathy, bath, load_sem.at[4]))
    loads += [
        pltpu.make_async_copy(x, whole.at[m], load_sem.at[5 + m]) for m, x in enumerate((wide, high, vort))
    ]
    for load in loads:
        load.start()

    barrier = pltpu.get_barrier_semaphore()
    for peer in (east, west, north):
        pl.semaphore_signal(barrier, inc=1, device_id=peer, device_id_type=MESH)

    @pl.when(lat > 0)
    def _():
        pl.semaphore_signal(barrier, inc=1, device_id=south, device_id_type=MESH)

    lane = lanes((8, width))
    row = lax.broadcasted_iota(jnp.int32, (8, width), 0)
    group = lane // 8
    within = lane - group * 8
    for load in loads:
        load.wait()

    @pl.loop(0, height // 8)
    def _(tile):
        start = pl.multiple_of(tile * 8, 8)
        rows = pl.ds(start, 8)
        cols = []
        for f in range(4):
            acc = pltpu.roll(field[f, rows, :], 8 * (levels - 1) + RIM, 1)
            for level in range(1, levels):
                spot = levels - 1 - level
                at = pl.ds(pl.multiple_of(start + level * height, 8), 8)
                acc = jnp.where(group == spot, pltpu.roll(field[f, at, :], 8 * spot + RIM, 1), acc)
            packed[f, rows, :] = acc
            cols.append(acc)
        acc = jnp.zeros((8, width), jnp.float32)
        raw = (bath[rows, :].astype(jnp.float32), whole[0, rows, :], whole[1, rows, :], whole[2, rows, :])
        for m in range(4):
            metric[m, rows, :] = raw[m]
            acc = jnp.where(group == m, pltpu.roll(raw[m], 8 * m + RIM, 1), acc)
        packed[4, rows, :] = acc
        for pair in range(2):
            one, two = cols[2 * pair], cols[2 * pair + 1]
            to_side[0, pair, rows, :] = jnp.where(within < 4, one, pltpu.roll(two, 4, 1))
            to_side[1, pair, rows, :] = jnp.where(within < 3, pltpu.roll(two, width - 3, 1), one)
        to_side[0, 2, rows, :] = acc
        to_side[1, 2, rows, :] = acc

    @pl.when(lat > 0)
    def _():
        pl.semaphore_wait(barrier, 4)

    @pl.when(lat == 0)
    def _():
        pl.semaphore_wait(barrier, 3)

    def remote(src, dst, which, arrive, peer):
        return pltpu.make_async_remote_copy(
            src_ref=src, dst_ref=dst, send_sem=send_sem.at[which], recv_sem=recv_sem.at[arrive],
            device_id=peer, device_id_type=MESH,
        )

    go_east = remote(to_side.at[0], from_side.at[0], 0, 0, east)
    go_west = remote(to_side.at[1], from_side.at[1], 1, 1, west)
    go_east.start()
    go_west.start()

    def column(f, r, half):
        return field[f, pl.ds(r + half * 8 * height, 8, stride=height), :]

    for f in range(4):
        for r in range(RIM):
            at = (f * RIM + r) * levels
            for half in range(levels // 8):
                rows = slice(at + 8 * half, at + 8 * half + 8)
                out_s[rows, :] = column(f, r, half)
                out_n[rows, :] = column(f, height - RIM + r, half)
    base = 4 * RIM * levels
    out_s[base : base + 16, :] = jnp.zeros((16, width), jnp.float32)
    out_n[base : base + 16, :] = jnp.zeros((16, width), jnp.float32)
    for m in range(4):
        out_s[base + m * RIM : base + (m + 1) * RIM, :] = metric[m, 0:RIM, :]
        out_n[base + m * RIM : base + (m + 1) * RIM, :] = metric[m, height - RIM : height, :]

    def rows_out(to_n, to_s, recv_n, recv_s, first):
        up = remote(to_n, recv_s, first, first, north)
        fold = remote(to_n, recv_n, first, first + 1, north)
        down = remote(to_s, recv_n, first + 1, first + 1, south)

        @pl.when(last)
        def _():
            fold.start()

        @pl.when(lat < lats - 1)
        def _():
            up.start()

        @pl.when(lat > 0)
        def _():
            down.start()

        return up, down

    def rows_in(up, down):
        down.wait_recv()

        @pl.when(lat > 0)
        def _():
            up.wait_recv()

    def rows_sent(up, down):
        up.wait_send()

        @pl.when(lat > 0)
        def _():
            down.wait_send()

    @pl.when(lat == 0)
    def _():
        rows_s[...] = jnp.zeros(rows_s.shape, jnp.float32)
        strip_s[...] = jnp.zeros(strip_s.shape, jnp.float32)

    main = rows_out(out_n, out_s, rows_n, rows_s, 2)

    @pl.loop(0, height // 8)
    def _(tile):
        rows = pl.ds(pl.multiple_of(tile * 8, 8), 8)
        made = factors(*[metric[m, rows, :] for m in range(4)])
        for m in range(6):
            for i in range(8):
                table[m, RIM + tile * 8 + i, :, :] = jnp.broadcast_to(made[m][i : i + 1, :], (8, width))

    def wet_of(at, half):
        return table[0, at, :, :] > (row + 8 * half).astype(jnp.float32)

    @pl.loop(0, height, unroll=2)
    def _(r):
        for half in range(levels // 8):
            wet = wet_of(RIM + r, half)
            for f in range(4):
                state[f, RIM + r, 8 * half : 8 * half + 8, :] = jnp.where(wet, column(f, r, half), 0.0)

    go_east.wait_recv()
    go_west.wait_recv()

    @pl.loop(0, height // 8)
    def _(tile):
        rows = pl.ds(pl.multiple_of(tile * 8, 8), 8)
        for f in range(5):
            own = packed[f, rows, :]
            got_w = from_side[0, f // 2, rows, :]
            got_e = from_side[1, f // 2, rows, :]
            if f % 2 == 1:
                got_w = pltpu.roll(got_w, width - 4, 1)
                got_e = pltpu.roll(got_e, 3, 1)
            strips[0, f, rows, :] = jnp.where(within < RIM, got_w, own)
            strips[1, f, rows, :] = jnp.where(within < RIM, own, got_e)

    edge_n[30:32, :] = jnp.zeros((2, width), jnp.float32)
    edge_s[30:32, :] = jnp.zeros((2, width), jnp.float32)
    for side in range(2):
        for f in range(5):
            at = (side * 5 + f) * RIM
            edge_s[at : at + RIM, :] = strips[side, f, 0:RIM, :]
            edge_n[at : at + RIM, :] = strips[side, f, height - RIM : height, :]
    ends = rows_out(edge_n, edge_s, strip_n, strip_s, 4)

    def side_tables(rows):
        for side in range(2):
            mixed = strips[side, 4, rows, :]
            spread = []
            for m in range(4):
                value = jnp.where(group == m, mixed, 0.0)
                for hop in (8, 16, 32, 64):
                    value = value + pltpu.roll(value, hop, 1)
                spread.append(value)
            made = factors(*spread)
            for m in range(6):
                side_metric[side, m, rows, :] = made[m]
            wet = made[0] > (levels - 1 - group).astype(jnp.float32)
            for f in range(4):
                sides[side, f, rows, :] = jnp.where(wet, strips[side, f, rows, :], 0.0)

    @pl.loop(0, height // 8)
    def _(tile):
        side_tables(pl.ds(pl.multiple_of(tile * 8, 8), 8))

    go_east.wait_send()
    go_west.wait_send()
    rows_in(*main)

    def mirrored(value, index):
        pieces = [
            jnp.take_along_axis(value[i : i + 8, :], index, axis=1)
            for i in range(0, value.shape[0], 8)
        ]
        return jnp.concatenate(pieces, axis=0)

    signs = (1.0, 1.0, -1.0, -1.0)
    safe = (0.0, 1.0, 1.0, 0.0)
    turn = width - 1 - lane
    far, near = rows_n[base : base + 16, :], rows_s[base : base + 16, :]
    flipped = mirrored(far, turn)
    for k in range(RIM):
        up = [
            jnp.where(
                last,
                flipped[m * RIM + RIM - 1 - k : m * RIM + RIM - k, :],
                far[m * RIM + k : m * RIM + k + 1, :],
            )
            for m in range(4)
        ]
        down = [
            jnp.where(bottom, safe[m], near[m * RIM + k : m * RIM + k + 1, :]) for m in range(4)
        ]
        for at, raw in ((RIM + height + k, up), (k, down)):
            made = factors(*raw)
            for m in range(6):
                table[m, at, :, :] = jnp.broadcast_to(made[m], (8, width))
        for half in range(levels // 8):
            wet_up, wet_down = wet_of(RIM + height + k, half), wet_of(k, half)
            for f in range(4):
                span = slice(8 * half, 8 * half + 8)
                at = (f * RIM + k) * levels + 8 * half
                fold = (f * RIM + RIM - 1 - k) * levels + 8 * half
                turned = signs[f] * jnp.take_along_axis(rows_n[fold : fold + 8, :], turn, axis=1)
                value = jnp.where(last, turned, rows_n[at : at + 8, :])
                state[f, RIM + height + k, span, :] = jnp.where(wet_up, value, 0.0)
                state[f, k, span, :] = jnp.where(wet_down, rows_s[at : at + 8, :], 0.0)

    rows_in(*ends)
    side_far = strip_n[...]
    side_flipped = mirrored(side_far, group * 8 + jnp.where(within < 6, 5 - within, within))
    side_near = strip_s[...]
    for side in range(2):
        for f in range(5):
            if f == 4:
                fill = jnp.where((group == 1) | (group == 2), 1.0, 0.0)
            else:
                fill = jnp.zeros((8, width), jnp.float32)
            strips[side, f, height:deep, :] = fill
            for r in range(RIM):
                at = (side * 5 + f) * RIM + r
                fold = ((1 - side) * 5 + f) * RIM + RIM - 1 - r
                sign = 1.0 if f == 4 else signs[f]
                strips[side, f, height + r : height + r + 1, :] = jnp.where(
                    last, sign * side_flipped[fold : fold + 1, :], side_far[at : at + 1, :]
                )
                got = side_near[at : at + 1, :]
                if f == 4:
                    got = jnp.where(bottom, fill[0:1, :], got)
                strips[side, f, deep - RIM + r : deep - RIM + r + 1, :] = got
    side_tables(slice(height, deep))
    rows_sent(*main)
    rows_sent(*ends)


def substeps(
    tracer_mix, momentum_mix, state, table, sides, side_metric,
    y0, y1, y2, y3,
    second, third, result, sides_second, sides_third, link, store_sem,
):
    outs = (y0, y1, y2, y3)
    rows_deep, levels, width = state.shape[1:]
    height = rows_deep - 2 * RIM
    halves = levels // 8
    tiles = sides.shape[2] // 8
    lane = lanes((8, width))
    row = lax.broadcasted_iota(jnp.int32, (8, width), 0)
    group = lane // 8
    within = lane - group * 8

    def levelled(mix, half):
        value = jnp.zeros((8, width), jnp.float32)
        for i in range(8):
            value = jnp.where(row == i, mix[8 * half + i], value)
        return value

    def grouped(mix):
        value = jnp.zeros((8, width), jnp.float32)
        for level in range(levels):
            value = jnp.where(group == levels - 1 - level, mix[level], value)
        return value

    mixes = [(levelled(tracer_mix, h), levelled(momentum_mix, h)) for h in range(halves)]
    numbers = [(row + 8 * h).astype(jnp.float32) for h in range(halves)]

    def update(centre, easts, wests, norths, souths, factor, number, mix):
        bath, a2, b2, ah, bh, vo = factor
        wet = bath > number
        a2 = jnp.where(wet, a2, 0.0)
        b2 = jnp.where(wet, b2, 0.0)
        u, v = centre[2], centre[3]
        du, dv = u * ah, v * bh
        results = []
        for f in range(4):
            if f % 2 == 0:
                da, db = mix[f // 2] * a2, mix[f // 2] * b2
                ce, cw, cn, cs = da - du, da + du, db - dv, db + dv
                cc = 1.0 - 2.0 * (da + db)
            new = cc * centre[f] + (ce * easts[f] + cw * wests[f])
            new = new + (cn * norths[f] + cs * souths[f])
            if f == 2:
                new = new + vo * v
            if f == 3:
                new = new - vo * u
            results.append(new)
        return results

    def main_step(source, store, low, high):
        @pl.loop(low, high, unroll=2)
        def _(r):
            factor = [table[m, r, :, :] for m in range(6)]
            seam_row = lax.rem(r + 8 * tiles - RIM, 8 * tiles)
            seams = [
                jnp.broadcast_to(link[f, pl.ds(seam_row, 1), :], (8, width)) for f in range(4)
            ]
            for half in range(halves):
                span = slice(8 * half, 8 * half + 8)
                centre = [source[f, r, span, :] for f in range(4)]
                easts, wests = [], []
                for f in range(4):
                    z = pltpu.roll(seams[f], width - 3 - 8 * (levels - 1) + 64 * half, 1, stride=8, stride_axis=0)
                    easts.append(pltpu.roll(jnp.where(lane == 0, z, centre[f]), width - 1, 1))
                    wests.append(pltpu.roll(jnp.where(lane == width - 1, z, centre[f]), 1, 1))
                norths = [source[f, r + 1, span, :] for f in range(4)]
                souths = [source[f, r - 1, span, :] for f in range(4)]
                new = update(centre, easts, wests, norths, souths, factor, numbers[half], mixes[half])
                for f in range(4):
                    store(f, r, half, new[f])

    def side_step(source, target):
        mix = (grouped(tracer_mix), grouped(momentum_mix))
        number = (levels - 1 - group).astype(jnp.float32)
        for side in range(2):
            for t in range(tiles):
                rows = slice(8 * t, 8 * t + 8)
                prior, following = (t + tiles - 1) % tiles * 8, (t + 1) % tiles * 8
                centre = [source[side, f, rows, :] for f in range(4)]
                easts = [pltpu.roll(c, width - 1, 1) for c in centre]
                wests = [pltpu.roll(c, 1, 1) for c in centre]
                norths = [
                    jnp.where(
                        row == 7,
                        pltpu.roll(source[side, f, following : following + 8, :], 7, 0),
                        pltpu.roll(centre[f], 7, 0),
                    )
                    for f in range(4)
                ]
                souths = [
                    jnp.where(
                        row == 0,
                        pltpu.roll(source[side, f, prior : prior + 8, :], 1, 0),
                        pltpu.roll(centre[f], 1, 0),
                    )
                    for f in range(4)
                ]
                factor = [side_metric[side, m, rows, :] for m in range(6)]
                new = update(centre, easts, wests, norths, souths, factor, number, mix)
                for f in range(4):
                    target[side, f, rows, :] = new[f]

    def join(source):
        for f in range(4):
            for t in range(tiles):
                rows = slice(8 * t, 8 * t + 8)
                link[f, rows, :] = jnp.where(within == 2, source[0, f, rows, :], source[1, f, rows, :])

    def into(buffer):
        def store(f, r, half, value):
            buffer[f, r, 8 * half : 8 * half + 8, :] = value
        return store

    def final(f, r, half, value):
        result[f, pl.ds(r - RIM + half * 8 * height, 8, stride=height), :] = value

    join(sides)
    main_step(state, into(second), 1, rows_deep - 1)
    side_step(sides, sides_second)
    join(sides_second)
    main_step(second, into(third), 2, rows_deep - 2)
    side_step(sides_second, sides_third)
    join(sides_third)
    main_step(third, final, 3, rows_deep - 3)
    stores = [
        pltpu.make_async_copy(result.at[f], outs[f], store_sem.at[f]) for f in range(4)
    ]
    for copy in stores:
        copy.start()
    for copy in stores:
        copy.wait()


def on_device(
    potential_heat_state,
    saltiness_anomaly,
    first_current_component,
    second_current_component,
    bathymetry_layer_total,
    westeast_cell_extent,
    southnorth_cell_extent,
    planetary_vorticity,
    scalar_mixing_factor,
    momentum_mixing_factor,
):
    fields = (potential_heat_state, saltiness_anomaly, first_current_component, second_current_component)
    metrics = (bathymetry_layer_total, westeast_cell_extent, southnorth_cell_extent, planetary_vorticity)
    levels, height, width = potential_heat_state.shape
    f32 = jnp.float32
    message = 4 * RIM * levels + 16
    deep = height + 8
    flat = (levels * height, width)
    vmem = pl.BlockSpec(memory_space=pltpu.VMEM)
    smem = pl.BlockSpec(memory_space=pltpu.SMEM)
    anywhere = pl.BlockSpec(memory_space=pltpu.HBM)
    laid = pl.pallas_call(
        exchange,
        out_shape=(
            pltpu.VMEM((4, height + 2 * RIM, levels, width), f32),
            pltpu.VMEM((6, height + 2 * RIM, 8, width), f32),
            pltpu.VMEM((2, 4, deep, width), f32),
            pltpu.VMEM((2, 6, deep, width), f32),
        ),
        in_specs=[anywhere] * 8,
        out_specs=[vmem] * 4,
        scratch_shapes=[
            pltpu.VMEM((4,) + flat, f32),
            pltpu.VMEM((3, height, width), f32),
            pltpu.VMEM((height, width), jnp.int32),
            pltpu.VMEM((4, height, width), f32),
            pltpu.VMEM((message, width), f32),
            pltpu.VMEM((message, width), f32),
            pltpu.VMEM((2, 5, deep, width), f32),
            pltpu.VMEM((32, width), f32),
            pltpu.VMEM((32, width), f32),
            pltpu.VMEM((message, width), f32),
            pltpu.VMEM((message, width), f32),
            pltpu.VMEM((5, height, width), f32),
            pltpu.VMEM((2, 3, height, width), f32),
            pltpu.VMEM((2, 3, height, width), f32),
            pltpu.VMEM((32, width), f32),
            pltpu.VMEM((32, width), f32),
            pltpu.SemaphoreType.DMA((6,)),
            pltpu.SemaphoreType.DMA((6,)),
            pltpu.SemaphoreType.DMA((8,)),
        ],
        compiler_params=pltpu.CompilerParams(
            collective_id=0, has_side_effects=True, vmem_limit_bytes=int(59.4 * 2**20)
        ),
        name="exchange",
    )(*[x.reshape(flat) for x in fields], *metrics)
    news = pl.pallas_call(
        substeps,
        out_shape=(jax.ShapeDtypeStruct(flat, f32),) * 4,
        in_specs=[smem] * 2 + [vmem] * 4,
        out_specs=[anywhere] * 4,
        scratch_shapes=[
            pltpu.VMEM((4, height + 2 * RIM, levels, width), f32),
            pltpu.VMEM((4, height + 2 * RIM, levels, width), f32),
            pltpu.VMEM((4,) + flat, f32),
            pltpu.VMEM((2, 4, deep, width), f32),
            pltpu.VMEM((2, 4, deep, width), f32),
            pltpu.VMEM((4, deep, width), f32),
            pltpu.SemaphoreType.DMA((4,)),
        ],
        compiler_params=pltpu.CompilerParams(vmem_limit_bytes=24 * 2**20),
        name="substeps",
    )(scalar_mixing_factor, momentum_mixing_factor, *laid)
    return tuple(x.reshape((levels, height, width)) for x in news)


def solution(mesh):
    state, plane = P(None, "lat", "lon"), P("lat", "lon")
    return jax.shard_map(
        on_device,
        mesh=mesh,
        in_specs=(state,) * 4 + (plane,) * 4 + (P(), P()),
        out_specs=(state,) * 4,
        check_vma=False,
    )
```

time: 38.6 us -> 38.8 us (level)
  the two profiles are of different devices: /device:TPU:13 before, /device:TPU:0 now
where the time goes in v2:
time: 38.8 us; the launch traced here: 38.4 us
  Pallas kernels  36.5 us (94%)
  local copies, waits for them, and re-layouts  1.31 us (3%)
  between operations  0.65 us (2%)
    pallas_call x1, Pallas kernels, on_device(): pl.pallas_call(substeps, out_shape=(jax.ShapeDtypeStruct(flat, f32),) * 4...  21.3 us
    pallas_call x1, Pallas kernels, on_device(): pl.pallas_call(exchange, out_shape=(pltpu.VMEM((4, height + 2 * RIM, leve...  15.2 us
    unnamed x4, local copies, waits for them, and re-layouts  1.31 us

profile of v2, /device:TPU:0, one launch (start us, length us, event | category | flops | bytes accessed | tf_op | source)
XLA Modules:
  0.0 38.4 jit_solution(1898874273887605981)
XLA Ops:
  0.6 15.2 %exchange.1 = (f32[4,70,16,128]{3,2,1,0:T(8,128)S(1)}, f32[6,70,8,128]{3,2,1,0:T(8,128)S(1)}, f32[2,4,72,128]{3,2,1,0:T(8,128)S(1)}, f32[2,6,72,128]{3,2,1,0:T(8,128)S(1)}) custom-call(f32[1024,128]{1,0:T(8,128)} %bitcast.8, f32[1024,128]{1,0:T(8,128)} %bitcast.9, f32[1024,128]{1,0:T(8,128)} %bitcast.10, f32[1024,128]{1,0:T(8,128)} %bitcast.11, ...), custom_call_target="tpu_custom_call" | custom-call | tf_op jit(solution)/shard_map/exchange/pallas_call | solution.py:469
  15.8 0.0 copy-start
  15.8 0.6 %copy-done = f32[16]{0:T(128)S(1)} copy-done((f32[16]{0:T(128)S(1)}, f32[16]{0:T(128)}, u32[]{:S(2)}) %copy-start) | copy-done | bytes 88
  16.5 0.0 copy-start.1
  16.5 0.7 %copy-done.1 = f32[16]{0:T(128)S(1)} copy-done((f32[16]{0:T(128)S(1)}, f32[16]{0:T(128)}, u32[]{:S(2)}) %copy-start.1) | copy-done | bytes 88
  17.1 21.3 %substeps.1 = (f32[1024,128]{1,0:T(8,128)}, f32[1024,128]{1,0:T(8,128)}, f32[1024,128]{1,0:T(8,128)}, f32[1024,128]{1,0:T(8,128)}) custom-call(f32[16]{0:T(128)S(1)} %copy-done, f32[16]{0:T(128)S(1)} %copy-done.1, f32[4,70,16,128]{3,2,1,0:T(8,128)S(1)} %get-tuple-element.12.state, f32[6,70,8,128]{3,2,1,0:T(8,128)S(1)} %get-tuple-element.13.table, ...), custom_call_target="tpu_custom_call" | custom-call | tf_op jit(solution)/shard_map/substeps/pallas_call | solution.py:505
Async XLA Ops:
  15.8 0.7 %copy-start = (f32[16]{0:T(128)S(1)}, f32[16]{0:T(128)}, u32[]{:S(2)}) copy-start(f32[16]{0:T(128)} %tracer_mix.1) | copy-start | bytes 196
  16.5 0.7 %copy-start.1 = (f32[16]{0:T(128)S(1)}, f32[16]{0:T(128)}, u32[]{:S(2)}) copy-start(f32[16]{0:T(128)} %momentum_mix.1) | copy-start | bytes 196

commit v3 on v2

--- a/solution.py
+++ b/solution.py
@@ -27,9 +27,9 @@
 
 
 def exchange(
-    x0, x1, x2, x3, bathy, wide, high, vort,
-    state, table, sides, side_metric,
-    field, whole, bath, metric,
+    x0, x1, x2, x3, bathy, wide, high, vort, tracer_mix, momentum_mix,
+    state, table, sides, side_metric, mixing,
+    factor_t, factor_m, field, whole, bath, metric,
     rows_n, rows_s, strips, strip_n, strip_s,
     out_n, out_s, packed, to_side, from_side, edge_n, edge_s,
     send_sem, recv_sem, load_sem,
@@ -54,6 +54,10 @@
     loads.append(pltpu.make_async_copy(bathy, bath, load_sem.at[4]))
     loads += [
         pltpu.make_async_copy(x, whole.at[m], load_sem.at[5 + m]) for m, x in enumerate((wide, high, vort))
+    ]
+    loads += [
+        pltpu.make_async_copy(tracer_mix, factor_t, load_sem.at[8]),
+        pltpu.make_async_copy(momentum_mix, factor_m, load_sem.at[9]),
     ]
     for load in loads:
         load.start()
@@ -186,13 +190,6 @@
     def wet_of(at, half):
         return table[0, at, :, :] > (row + 8 * half).astype(jnp.float32)
 
-    @pl.loop(0, height, unroll=2)
-    def _(r):
-        for half in range(levels // 8):
-            wet = wet_of(RIM + r, half)
-            for f in range(4):
-                state[f, RIM + r, 8 * half : 8 * half + 8, :] = jnp.where(wet, column(f, r, half), 0.0)
-
     go_east.wait_recv()
     go_west.wait_recv()
 
@@ -217,6 +214,23 @@
             edge_s[at : at + RIM, :] = strips[side, f, 0:RIM, :]
             edge_n[at : at + RIM, :] = strips[side, f, height - RIM : height, :]
     ends = rows_out(edge_n, edge_s, strip_n, strip_s, 4)
+
+    @pl.loop(0, height, unroll=8)
+    def _(r):
+        for half in range(levels // 8):
+            wet = wet_of(RIM + r, half)
+            for f in range(4):
+                state[f, RIM + r, 8 * half : 8 * half + 8, :] = jnp.where(wet, column(f, r, half), 0.0)
+
+    for k, mix in enumerate((factor_t, factor_m)):
+        spread = jnp.zeros((8, width), jnp.float32)
+        for half in range(levels // 8):
+            value = jnp.zeros((8, width), jnp.float32)
+            for i in range(8):
+                value = jnp.where(row == i, mix[8 * half + i], value)
+                spread = jnp.where(group == levels - 1 - 8 * half - i, mix[8 * half + i], spread)
+            mixing[(levels // 8 + 1) * k + half] = value
+        mixing[(levels // 8 + 1) * k + levels // 8] = spread
 
     def side_tables(rows):
         for side in range(2):
@@ -309,7 +323,7 @@
 
 
 def substeps(
-    tracer_mix, momentum_mix, state, table, sides, side_metric,
+    state, table, sides, side_metric, mixing,
     y0, y1, y2, y3,
     second, third, result, sides_second, sides_third, link, store_sem,
 ):
@@ -323,19 +337,7 @@
     group = lane // 8
     within = lane - group * 8
 
-    def levelled(mix, half):
-        value = jnp.zeros((8, width), jnp.float32)
-        for i in range(8):
-            value = jnp.where(row == i, mix[8 * half + i], value)
-        return value
-
-    def grouped(mix):
-        value = jnp.zeros((8, width), jnp.float32)
-        for level in range(levels):
-            value = jnp.where(group == levels - 1 - level, mix[level], value)
-        return value
-
-    mixes = [(levelled(tracer_mix, h), levelled(momentum_mix, h)) for h in range(halves)]
+    mixes = [(mixing[h], mixing[halves + 1 + h]) for h in range(halves)]
     numbers = [(row + 8 * h).astype(jnp.float32) for h in range(halves)]
 
     def update(centre, easts, wests, norths, souths, factor, number, mix):
@@ -360,8 +362,8 @@
             results.append(new)
         return results
 
-    def main_step(source, store, low, high):
-        @pl.loop(low, high, unroll=2)
+    def main_step(source, store, low, high, unroll):
+        @pl.loop(low, high, unroll=unroll)
         def _(r):
             factor = [table[m, r, :, :] for m in range(6)]
             seam_row = lax.rem(r + 8 * tiles - RIM, 8 * tiles)
@@ -383,7 +385,7 @@
                     store(f, r, half, new[f])
 
     def side_step(source, target):
-        mix = (grouped(tracer_mix), grouped(momentum_mix))
+        mix = (mixing[halves], mixing[2 * halves + 1])
         number = (levels - 1 - group).astype(jnp.float32)
         for side in range(2):
             for t in range(tiles):
@@ -427,14 +429,17 @@
     def final(f, r, half, value):
         result[f, pl.ds(r - RIM + half * 8 * height, 8, stride=height), :] = value
 
+    def split(count):
+        return max(n for n in range(1, 18) if count % n == 0)
+
     join(sides)
-    main_step(state, into(second), 1, rows_deep - 1)
+    main_step(state, into(second), 1, rows_deep - 1, split(rows_deep - 2))
     side_step(sides, sides_second)
     join(sides_second)
-    main_step(second, into(third), 2, rows_deep - 2)
+    main_step(second, into(third), 2, rows_deep - 2, split(rows_deep - 4))
     side_step(sides_second, sides_third)
     join(sides_third)
-    main_step(third, final, 3, rows_deep - 3)
+    main_step(third, final, 3, rows_deep - 3, split(rows_deep - 6))
     stores = [
         pltpu.make_async_copy(result.at[f], outs[f], store_sem.at[f]) for f in range(4)
     ]
@@ -464,7 +469,6 @@
     deep = height + 8
     flat = (levels * height, width)
     vmem = pl.BlockSpec(memory_space=pltpu.VMEM)
-    smem = pl.BlockSpec(memory_space=pltpu.SMEM)
     anywhere = pl.BlockSpec(memory_space=pltpu.HBM)
     laid = pl.pallas_call(
         exchange,
@@ -473,10 +477,13 @@
             pltpu.VMEM((6, height + 2 * RIM, 8, width), f32),
             pltpu.VMEM((2, 4, deep, width), f32),
             pltpu.VMEM((2, 6, deep, width), f32),
+            pltpu.VMEM((2 * (levels // 8 + 1), 8, width), f32),
         ),
-        in_specs=[anywhere] * 8,
-        out_specs=[vmem] * 4,
+        in_specs=[anywhere] * 10,
+        out_specs=[vmem] * 5,
         scratch_shapes=[
+            pltpu.SMEM((levels,), f32),
+            pltpu.SMEM((levels,), f32),
             pltpu.VMEM((4,) + flat, f32),
             pltpu.VMEM((3, height, width), f32),
             pltpu.VMEM((height, width), jnp.int32),
@@ -495,17 +502,17 @@
             pltpu.VMEM((32, width), f32),
             pltpu.SemaphoreType.DMA((6,)),
             pltpu.SemaphoreType.DMA((6,)),
-            pltpu.SemaphoreType.DMA((8,)),
+            pltpu.SemaphoreType.DMA((10,)),
         ],
         compiler_params=pltpu.CompilerParams(
-            collective_id=0, has_side_effects=True, vmem_limit_bytes=int(59.4 * 2**20)
+            collective_id=0, has_side_effects=True, vmem_limit_bytes=int(59.36 * 2**20)
         ),
         name="exchange",
-    )(*[x.reshape(flat) for x in fields], *metrics)
+    )(*[x.reshape(flat) for x in fields], *metrics, scalar_mixing_factor, momentum_mixing_factor)
     news = pl.pallas_call(
         substeps,
         out_shape=(jax.ShapeDtypeStruct(flat, f32),) * 4,
-        in_specs=[smem] * 2 + [vmem] * 4,
+        in_specs=[vmem] * 5,
         out_specs=[anywhere] * 4,
         scratch_shapes=[
             pltpu.VMEM((4, height + 2 * RIM, levels, width), f32),
@@ -518,7 +525,7 @@
         ],
         compiler_params=pltpu.CompilerParams(vmem_limit_bytes=24 * 2**20),
         name="substeps",
-    )(scalar_mixing_factor, momentum_mixing_factor, *laid)
+    )(*laid)
     return tuple(x.reshape((levels, height, width)) for x in news)
 
 

time: 38.8 us -> 87.2 us (2.25)
  Pallas kernels: 36.5 us -> 86.4 us
  local copies, waits for them, and re-layouts: 1.31 us -> 0 us
    pallas_call x1, Pallas kernels: 21.3 us -> 69.6 us  [on_device(): pl.pallas_call(substeps, out_shape=(jax.ShapeDtypeStruct(flat, f32),) * 4...]
    pallas_call x1, Pallas kernels: 15.2 us -> 16.8 us  [on_device(): pl.pallas_call(exchange, out_shape=(pltpu.VMEM((4, height + 2 * RIM, leve...]
    unnamed x4 -> x0, local copies, waits for them, and re-layouts: 1.31 us -> none
where the time goes in v3:
time: 87.2 us; the launch traced here: 87 us
  Pallas kernels  86.4 us (99%)
    pallas_call x1, Pallas kernels, on_device(): pl.pallas_call(substeps, out_shape=(jax.ShapeDtypeStruct(flat, f32),) * 4...  69.6 us
    pallas_call x1, Pallas kernels, on_device(): pl.pallas_call(exchange, out_shape=(pltpu.VMEM((4, height + 2 * RIM, leve...  16.8 us

profile of v3, /device:TPU:0, one launch (start us, length us, event | category | flops | bytes accessed | tf_op | source)
XLA Modules:
  0.0 87.0 jit_solution(17945325032164870289)
XLA Ops:
  0.6 16.8 %exchange.1 = (f32[4,70,16,128]{3,2,1,0:T(8,128)S(1)}, f32[6,70,8,128]{3,2,1,0:T(8,128)S(1)}, f32[2,4,72,128]{3,2,1,0:T(8,128)S(1)}, f32[2,6,72,128]{3,2,1,0:T(8,128)S(1)}, f32[6,8,128]{2,1,0:T(8,128)S(1)}) custom-call(f32[1024,128]{1,0:T(8,128)} %bitcast.8, f32[1024,128]{1,0:T(8,128)} %bitcast.9, f32[1024,128]{1,0:T(8,128)} %bitcast.10, ...), custom_call_target="tpu_custom_call" | custom-call | tf_op jit(solution)/shard_map/exchange/pallas_call | solution.py:473
  17.4 69.6 %substeps.1 = (f32[1024,128]{1,0:T(8,128)}, f32[1024,128]{1,0:T(8,128)}, f32[1024,128]{1,0:T(8,128)}, f32[1024,128]{1,0:T(8,128)}) custom-call(f32[4,70,16,128]{3,2,1,0:T(8,128)S(1)} %get-tuple-element.13.state, f32[6,70,8,128]{3,2,1,0:T(8,128)S(1)} %get-tuple-element.14.table, f32[2,4,72,128]{3,2,1,0:T(8,128)S(1)} %get-tuple-element.15.sides, ...), custom_call_target="tpu_custom_call" | custom-call | tf_op jit(solution)/shard_map/substeps/pallas_call | solution.py:512

commit v4 on v3

--- a/solution.py
+++ b/solution.py
@@ -325,7 +325,7 @@
 def substeps(
     state, table, sides, side_metric, mixing,
     y0, y1, y2, y3,
-    second, third, result, sides_second, sides_third, link, store_sem,
+    second, third, result, sides_second, sides_third, seam, easts, wests, store_sem,
 ):
     outs = (y0, y1, y2, y3)
     rows_deep, levels, width = state.shape[1:]
@@ -362,25 +362,31 @@
             results.append(new)
         return results
 
-    def main_step(source, store, low, high, unroll):
-        @pl.loop(low, high, unroll=unroll)
+    def main_step(source, store, low, high):
+        @pl.loop(low, high, unroll=2)
+        def _(r):
+            seam_row = lax.rem(r + 8 * tiles - RIM, 8 * tiles) * levels
+            for half in range(halves):
+                span = slice(8 * half, 8 * half + 8)
+                place = pl.ds(pl.multiple_of(seam_row + 8 * half, 8), 8)
+                for f in range(4):
+                    z, c = seam[f, place, :], source[f, r, span, :]
+                    easts[f, r, span, :] = pltpu.roll(jnp.where(lane == 0, z, c), width - 1, 1)
+                    wests[f, r, span, :] = pltpu.roll(jnp.where(lane == width - 1, z, c), 1, 1)
+
+        @pl.loop(low, high)
         def _(r):
             factor = [table[m, r, :, :] for m in range(6)]
-            seam_row = lax.rem(r + 8 * tiles - RIM, 8 * tiles)
-            seams = [
-                jnp.broadcast_to(link[f, pl.ds(seam_row, 1), :], (8, width)) for f in range(4)
-            ]
             for half in range(halves):
                 span = slice(8 * half, 8 * half + 8)
-                centre = [source[f, r, span, :] for f in range(4)]
-                easts, wests = [], []
-                for f in range(4):
-                    z = pltpu.roll(seams[f], width - 3 - 8 * (levels - 1) + 64 * half, 1, stride=8, stride_axis=0)
-                    easts.append(pltpu.roll(jnp.where(lane == 0, z, centre[f]), width - 1, 1))
-                    wests.append(pltpu.roll(jnp.where(lane == width - 1, z, centre[f]), 1, 1))
-                norths = [source[f, r + 1, span, :] for f in range(4)]
-                souths = [source[f, r - 1, span, :] for f in range(4)]
-                new = update(centre, easts, wests, norths, souths, factor, numbers[half], mixes[half])
+                new = update(
+                    [source[f, r, span, :] for f in range(4)],
+                    [easts[f, r, span, :] for f in range(4)],
+                    [wests[f, r, span, :] for f in range(4)],
+                    [source[f, r + 1, span, :] for f in range(4)],
+                    [source[f, r - 1, span, :] for f in range(4)],
+                    factor, numbers[half], mixes[half],
+                )
                 for f in range(4):
                     store(f, r, half, new[f])
 
@@ -416,10 +422,15 @@
                     target[side, f, rows, :] = new[f]
 
     def join(source):
-        for f in range(4):
-            for t in range(tiles):
-                rows = slice(8 * t, 8 * t + 8)
-                link[f, rows, :] = jnp.where(within == 2, source[0, f, rows, :], source[1, f, rows, :])
+        @pl.loop(0, tiles)
+        def _(t):
+            rows = pl.ds(pl.multiple_of(t * 8, 8), 8)
+            for f in range(4):
+                z = jnp.where(within == 2, source[0, f, rows, :], source[1, f, rows, :])
+                for level in range(levels):
+                    spot = 8 * (levels - 1 - level) + 2
+                    moved = pltpu.roll(z, width - 1 - spot, 1)
+                    seam[f, pl.ds(t * 8 * levels + level, 8, stride=levels), :] = moved
 
     def into(buffer):
         def store(f, r, half, value):
@@ -429,17 +440,14 @@
     def final(f, r, half, value):
         result[f, pl.ds(r - RIM + half * 8 * height, 8, stride=height), :] = value
 
-    def split(count):
-        return max(n for n in range(1, 18) if count % n == 0)
-
     join(sides)
-    main_step(state, into(second), 1, rows_deep - 1, split(rows_deep - 2))
+    main_step(state, into(second), 1, rows_deep - 1)
     side_step(sides, sides_second)
     join(sides_second)
-    main_step(second, into(third), 2, rows_deep - 2, split(rows_deep - 4))
+    main_step(second, into(third), 2, rows_deep - 2)
     side_step(sides_second, sides_third)
     join(sides_third)
-    main_step(third, final, 3, rows_deep - 3, split(rows_deep - 6))
+    main_step(third, final, 3, rows_deep - 3)
     stores = [
         pltpu.make_async_copy(result.at[f], outs[f], store_sem.at[f]) for f in range(4)
     ]
@@ -520,10 +528,12 @@
             pltpu.VMEM((4,) + flat, f32),
             pltpu.VMEM((2, 4, deep, width), f32),
             pltpu.VMEM((2, 4, deep, width), f32),
-            pltpu.VMEM((4, deep, width), f32),
+            pltpu.VMEM((4, deep * levels, width), f32),
+            pltpu.VMEM((4, height + 2 * RIM, levels, width), f32),
+            pltpu.VMEM((4, height + 2 * RIM, levels, width), f32),
             pltpu.SemaphoreType.DMA((4,)),
         ],
-        compiler_params=pltpu.CompilerParams(vmem_limit_bytes=24 * 2**20),
+        compiler_params=pltpu.CompilerParams(vmem_limit_bytes=32 * 2**20),
         name="substeps",
     )(*laid)
     return tuple(x.reshape((levels, height, width)) for x in news)

time: 87.2 us -> 39.6 us (0.45)
  Pallas kernels: 86.4 us -> 38.8 us
    pallas_call x1, Pallas kernels: 69.6 us -> 22 us  [on_device(): pl.pallas_call(substeps, out_shape=(jax.ShapeDtypeStruct(flat, f32),) * 4...]
where the time goes in v4:
time: 39.6 us; the launch traced here: 39.4 us
  Pallas kernels  38.8 us (98%)
  between operations  0.64 us (2%)
    pallas_call x1, Pallas kernels, on_device(): pl.pallas_call(substeps, out_shape=(jax.ShapeDtypeStruct(flat, f32),) * 4...  22 us
    pallas_call x1, Pallas kernels, on_device(): pl.pallas_call(exchange, out_shape=(pltpu.VMEM((4, height + 2 * RIM, leve...  16.8 us

profile of v4, /device:TPU:0, one launch (start us, length us, event | category | flops | bytes accessed | tf_op | source)
XLA Modules:
  0.0 39.4 jit_solution(17261438668967121323)
XLA Ops:
  0.6 16.8 %exchange.1 = (f32[4,70,16,128]{3,2,1,0:T(8,128)S(1)}, f32[6,70,8,128]{3,2,1,0:T(8,128)S(1)}, f32[2,4,72,128]{3,2,1,0:T(8,128)S(1)}, f32[2,6,72,128]{3,2,1,0:T(8,128)S(1)}, f32[6,8,128]{2,1,0:T(8,128)S(1)}) custom-call(f32[1024,128]{1,0:T(8,128)} %bitcast.8, f32[1024,128]{1,0:T(8,128)} %bitcast.9, f32[1024,128]{1,0:T(8,128)} %bitcast.10, ...), custom_call_target="tpu_custom_call" | custom-call | tf_op jit(solution)/shard_map/exchange/pallas_call | solution.py:481
  17.4 22.0 %substeps.1 = (f32[1024,128]{1,0:T(8,128)}, f32[1024,128]{1,0:T(8,128)}, f32[1024,128]{1,0:T(8,128)}, f32[1024,128]{1,0:T(8,128)}) custom-call(f32[4,70,16,128]{3,2,1,0:T(8,128)S(1)} %get-tuple-element.13.state, f32[6,70,8,128]{3,2,1,0:T(8,128)S(1)} %get-tuple-element.14.table, f32[2,4,72,128]{3,2,1,0:T(8,128)S(1)} %get-tuple-element.15.sides, ...), custom_call_target="tpu_custom_call" | custom-call | tf_op jit(solution)/shard_map/substeps/pallas_call | solution.py:520

commit v5 on v3

--- a/solution.py
+++ b/solution.py
@@ -34,7 +34,7 @@
     out_n, out_s, packed, to_side, from_side, edge_n, edge_s,
     send_sem, recv_sem, load_sem,
 ):
-    levels, width = state.shape[2], state.shape[3]
+    levels, width = state.shape[1], state.shape[3]
     height = wide.shape[0]
     deep = height + 8
     lat, lon = lax.axis_index("lat"), lax.axis_index("lon")
@@ -184,11 +184,7 @@
         rows = pl.ds(pl.multiple_of(tile * 8, 8), 8)
         made = factors(*[metric[m, rows, :] for m in range(4)])
         for m in range(6):
-            for i in range(8):
-                table[m, RIM + tile * 8 + i, :, :] = jnp.broadcast_to(made[m][i : i + 1, :], (8, width))
-
-    def wet_of(at, half):
-        return table[0, at, :, :] > (row + 8 * half).astype(jnp.float32)
+            table[m, rows, :] = made[m]
 
     go_east.wait_recv()
     go_west.wait_recv()
@@ -215,22 +211,21 @@
             edge_n[at : at + RIM, :] = strips[side, f, height - RIM : height, :]
     ends = rows_out(edge_n, edge_s, strip_n, strip_s, 4)
 
-    @pl.loop(0, height, unroll=8)
-    def _(r):
-        for half in range(levels // 8):
-            wet = wet_of(RIM + r, half)
+    @pl.loop(0, levels)
+    def _(level):
+        number = level.astype(jnp.float32)
+        for t in range(height // 8):
+            wet = table[0, 8 * t : 8 * t + 8, :] > number
+            at = pl.ds(pl.multiple_of(level * height + 8 * t, 8), 8)
             for f in range(4):
-                state[f, RIM + r, 8 * half : 8 * half + 8, :] = jnp.where(wet, column(f, r, half), 0.0)
+                state[f, level, 8 * t : 8 * t + 8, :] = jnp.where(wet, field[f, at, :], 0.0)
 
     for k, mix in enumerate((factor_t, factor_m)):
         spread = jnp.zeros((8, width), jnp.float32)
-        for half in range(levels // 8):
-            value = jnp.zeros((8, width), jnp.float32)
-            for i in range(8):
-                value = jnp.where(row == i, mix[8 * half + i], value)
-                spread = jnp.where(group == levels - 1 - 8 * half - i, mix[8 * half + i], spread)
-            mixing[(levels // 8 + 1) * k + half] = value
-        mixing[(levels // 8 + 1) * k + levels // 8] = spread
+        for level in range(levels):
+            spread = jnp.where(group == levels - 1 - level, mix[level], spread)
+            mixing[k, level] = jnp.full((8, width), mix[level], jnp.float32)
+        mixing[k, levels] = spread
 
     def side_tables(rows):
         for side in range(2):
@@ -268,32 +263,33 @@
     turn = width - 1 - lane
     far, near = rows_n[base : base + 16, :], rows_s[base : base + 16, :]
     flipped = mirrored(far, turn)
-    for k in range(RIM):
-        up = [
-            jnp.where(
-                last,
-                flipped[m * RIM + RIM - 1 - k : m * RIM + RIM - k, :],
-                far[m * RIM + k : m * RIM + k + 1, :],
+    for m in range(4):
+        metric[m, height:deep, :] = jnp.full((8, width), safe[m], jnp.float32)
+        for k in range(RIM):
+            at, fold = m * RIM + k, m * RIM + RIM - 1 - k
+            metric[m, height + k : height + k + 1, :] = jnp.where(
+                last, flipped[fold : fold + 1, :], far[at : at + 1, :]
             )
-            for m in range(4)
-        ]
-        down = [
-            jnp.where(bottom, safe[m], near[m * RIM + k : m * RIM + k + 1, :]) for m in range(4)
-        ]
-        for at, raw in ((RIM + height + k, up), (k, down)):
-            made = factors(*raw)
-            for m in range(6):
-                table[m, at, :, :] = jnp.broadcast_to(made[m], (8, width))
-        for half in range(levels // 8):
-            wet_up, wet_down = wet_of(RIM + height + k, half), wet_of(k, half)
-            for f in range(4):
-                span = slice(8 * half, 8 * half + 8)
-                at = (f * RIM + k) * levels + 8 * half
-                fold = (f * RIM + RIM - 1 - k) * levels + 8 * half
-                turned = signs[f] * jnp.take_along_axis(rows_n[fold : fold + 8, :], turn, axis=1)
-                value = jnp.where(last, turned, rows_n[at : at + 8, :])
-                state[f, RIM + height + k, span, :] = jnp.where(wet_up, value, 0.0)
-                state[f, k, span, :] = jnp.where(wet_down, rows_s[at : at + 8, :], 0.0)
+            metric[m, deep - RIM + k : deep - RIM + k + 1, :] = jnp.where(
+                bottom, safe[m], near[at : at + 1, :]
+            )
+    made = factors(*[metric[m, height:deep, :] for m in range(4)])
+    for m in range(6):
+        table[m, height:deep, :] = made[m]
+    for f in range(4):
+        for k in range(RIM):
+            at = (f * RIM + k) * levels
+            fold = (f * RIM + RIM - 1 - k) * levels
+            turned = signs[f] * mirrored(rows_n[fold : fold + levels, :], turn)
+            state[f, :, height + k, :] = jnp.where(last, turned, rows_n[at : at + levels, :])
+            state[f, :, deep - RIM + k, :] = rows_s[at : at + levels, :]
+    rim = (row < RIM) | (row >= 8 - RIM)
+
+    @pl.loop(0, levels)
+    def _(level):
+        wet = rim & (table[0, height:deep, :] > level.astype(jnp.float32))
+        for f in range(4):
+            state[f, level, height:deep, :] = jnp.where(wet, state[f, level, height:deep, :], 0.0)
 
     rows_in(*ends)
     side_far = strip_n[...]
@@ -328,17 +324,12 @@
     second, third, result, sides_second, sides_third, link, store_sem,
 ):
     outs = (y0, y1, y2, y3)
-    rows_deep, levels, width = state.shape[1:]
-    height = rows_deep - 2 * RIM
-    halves = levels // 8
-    tiles = sides.shape[2] // 8
+    levels, deep, width = state.shape[1:]
+    tiles = deep // 8
     lane = lanes((8, width))
     row = lax.broadcasted_iota(jnp.int32, (8, width), 0)
     group = lane // 8
     within = lane - group * 8
-
-    mixes = [(mixing[h], mixing[halves + 1 + h]) for h in range(halves)]
-    numbers = [(row + 8 * h).astype(jnp.float32) for h in range(halves)]
 
     def update(centre, easts, wests, norths, souths, factor, number, mix):
         bath, a2, b2, ah, bh, vo = factor
@@ -362,42 +353,51 @@
             results.append(new)
         return results
 
-    def main_step(source, store, low, high, unroll):
-        @pl.loop(low, high, unroll=unroll)
-        def _(r):
-            factor = [table[m, r, :, :] for m in range(6)]
-            seam_row = lax.rem(r + 8 * tiles - RIM, 8 * tiles)
-            seams = [
-                jnp.broadcast_to(link[f, pl.ds(seam_row, 1), :], (8, width)) for f in range(4)
-            ]
-            for half in range(halves):
-                span = slice(8 * half, 8 * half + 8)
-                centre = [source[f, r, span, :] for f in range(4)]
-                easts, wests = [], []
+    def main_step(source, store, count):
+        @pl.loop(0, levels)
+        def _(level):
+            number = level.astype(jnp.float32)
+            mix = (mixing[0, level], mixing[1, level])
+            for t in range(count):
+                rows = slice(8 * t, 8 * t + 8)
+                centre, easts, wests, norths, souths = [], [], [], [], []
                 for f in range(4):
-                    z = pltpu.roll(seams[f], width - 3 - 8 * (levels - 1) + 64 * half, 1, stride=8, stride_axis=0)
-                    easts.append(pltpu.roll(jnp.where(lane == 0, z, centre[f]), width - 1, 1))
-                    wests.append(pltpu.roll(jnp.where(lane == width - 1, z, centre[f]), 1, 1))
-                norths = [source[f, r + 1, span, :] for f in range(4)]
-                souths = [source[f, r - 1, span, :] for f in range(4)]
-                new = update(centre, easts, wests, norths, souths, factor, numbers[half], mixes[half])
+                    c = source[f, level, rows, :]
+                    z = pltpu.roll(link[f, rows, :], width - 3 - 8 * (levels - 1) + 8 * level, 1)
+                    centre.append(c)
+                    easts.append(pltpu.roll(jnp.where(lane == 0, z, c), width - 1, 1))
+                    wests.append(pltpu.roll(jnp.where(lane == width - 1, z, c), 1, 1))
+                    if t < tiles - 1:
+                        norths.append(source[f, level, 8 * t + 1 : 8 * t + 9, :])
+                    else:
+                        wrapped = pltpu.roll(source[f, level, 0:8, :], 7, 0)
+                        norths.append(jnp.where(row == 7, wrapped, pltpu.roll(c, 7, 0)))
+                    if t > 0:
+                        souths.append(source[f, level, 8 * t - 1 : 8 * t + 7, :])
+                    else:
+                        wrapped = pltpu.roll(source[f, level, deep - 8 : deep, :], 1, 0)
+                        souths.append(jnp.where(row == 0, wrapped, pltpu.roll(c, 1, 0)))
+                factor = [table[m, rows, :] for m in range(6)]
+                new = update(centre, easts, wests, norths, souths, factor, number, mix)
                 for f in range(4):
-                    store(f, r, half, new[f])
+                    store(f, level, t, new[f])
 
     def side_step(source, target):
-        mix = (mixing[halves], mixing[2 * halves + 1])
+        mix = (mixing[0, levels], mixing[1, levels])
         number = (levels - 1 - group).astype(jnp.float32)
-        for side in range(2):
-            for t in range(tiles):
-                rows = slice(8 * t, 8 * t + 8)
-                prior, following = (t + tiles - 1) % tiles * 8, (t + 1) % tiles * 8
+        @pl.loop(0, tiles)
+        def _(t):
+            rows = pl.ds(pl.multiple_of(8 * t, 8), 8)
+            prior = pl.ds(pl.multiple_of(lax.rem(t + tiles - 1, tiles) * 8, 8), 8)
+            following = pl.ds(pl.multiple_of(lax.rem(t + 1, tiles) * 8, 8), 8)
+            for side in range(2):
                 centre = [source[side, f, rows, :] for f in range(4)]
                 easts = [pltpu.roll(c, width - 1, 1) for c in centre]
                 wests = [pltpu.roll(c, 1, 1) for c in centre]
                 norths = [
                     jnp.where(
                         row == 7,
-                        pltpu.roll(source[side, f, following : following + 8, :], 7, 0),
+                        pltpu.roll(source[side, f, following, :], 7, 0),
                         pltpu.roll(centre[f], 7, 0),
                     )
                     for f in range(4)
@@ -405,7 +405,7 @@
                 souths = [
                     jnp.where(
                         row == 0,
-                        pltpu.roll(source[side, f, prior : prior + 8, :], 1, 0),
+                        pltpu.roll(source[side, f, prior, :], 1, 0),
                         pltpu.roll(centre[f], 1, 0),
                     )
                     for f in range(4)
@@ -416,30 +416,28 @@
                     target[side, f, rows, :] = new[f]
 
     def join(source):
-        for f in range(4):
-            for t in range(tiles):
-                rows = slice(8 * t, 8 * t + 8)
+        @pl.loop(0, tiles)
+        def _(t):
+            rows = pl.ds(pl.multiple_of(t * 8, 8), 8)
+            for f in range(4):
                 link[f, rows, :] = jnp.where(within == 2, source[0, f, rows, :], source[1, f, rows, :])
 
     def into(buffer):
-        def store(f, r, half, value):
-            buffer[f, r, 8 * half : 8 * half + 8, :] = value
+        def store(f, level, t, value):
+            buffer[f, level, 8 * t : 8 * t + 8, :] = value
         return store
 
-    def final(f, r, half, value):
-        result[f, pl.ds(r - RIM + half * 8 * height, 8, stride=height), :] = value
-
-    def split(count):
-        return max(n for n in range(1, 18) if count % n == 0)
+    def final(f, level, t, value):
+        result[f, level, 8 * t : 8 * t + 8, :] = value
 
     join(sides)
-    main_step(state, into(second), 1, rows_deep - 1, split(rows_deep - 2))
+    main_step(state, into(second), tiles)
     side_step(sides, sides_second)
     join(sides_second)
-    main_step(second, into(third), 2, rows_deep - 2, split(rows_deep - 4))
+    main_step(second, into(third), tiles)
     side_step(sides_second, sides_third)
     join(sides_third)
-    main_step(third, final, 3, rows_deep - 3, split(rows_deep - 6))
+    main_step(third, final, tiles - 1)
     stores = [
         pltpu.make_async_copy(result.at[f], outs[f], store_sem.at[f]) for f in range(4)
     ]
@@ -473,11 +471,11 @@
     laid = pl.pallas_call(
         exchange,
         out_shape=(
-            pltpu.VMEM((4, height + 2 * RIM, levels, width), f32),
-            pltpu.VMEM((6, height + 2 * RIM, 8, width), f32),
+            pltpu.VMEM((4, levels, deep, width), f32),
+            pltpu.VMEM((6, deep, width), f32),
             pltpu.VMEM((2, 4, deep, width), f32),
             pltpu.VMEM((2, 6, deep, width), f32),
-            pltpu.VMEM((2 * (levels // 8 + 1), 8, width), f32),
+            pltpu.VMEM((2, levels + 1, 8, width), f32),
         ),
         in_specs=[anywhere] * 10,
         out_specs=[vmem] * 5,
@@ -487,7 +485,7 @@
             pltpu.VMEM((4,) + flat, f32),
             pltpu.VMEM((3, height, width), f32),
             pltpu.VMEM((height, width), jnp.int32),
-            pltpu.VMEM((4, height, width), f32),
+            pltpu.VMEM((4, deep, width), f32),
             pltpu.VMEM((message, width), f32),
             pltpu.VMEM((message, width), f32),
             pltpu.VMEM((2, 5, deep, width), f32),
@@ -505,28 +503,28 @@
             pltpu.SemaphoreType.DMA((10,)),
         ],
         compiler_params=pltpu.CompilerParams(
-            collective_id=0, has_side_effects=True, vmem_limit_bytes=int(59.36 * 2**20)
+            collective_id=0, has_side_effects=True, vmem_limit_bytes=int(60.6 * 2**20)
         ),
         name="exchange",
     )(*[x.reshape(flat) for x in fields], *metrics, scalar_mixing_factor, momentum_mixing_factor)
     news = pl.pallas_call(
         substeps,
-        out_shape=(jax.ShapeDtypeStruct(flat, f32),) * 4,
+        out_shape=(jax.ShapeDtypeStruct((levels, height, width), f32),) * 4,
         in_specs=[vmem] * 5,
         out_specs=[anywhere] * 4,
         scratch_shapes=[
-            pltpu.VMEM((4, height + 2 * RIM, levels, width), f32),
-            pltpu.VMEM((4, height + 2 * RIM, levels, width), f32),
-            pltpu.VMEM((4,) + flat, f32),
+            pltpu.VMEM((4, levels, deep, width), f32),
+            pltpu.VMEM((4, levels, deep, width), f32),
+            pltpu.VMEM((4, levels, height, width), f32),
             pltpu.VMEM((2, 4, deep, width), f32),
             pltpu.VMEM((2, 4, deep, width), f32),
             pltpu.VMEM((4, deep, width), f32),
             pltpu.SemaphoreType.DMA((4,)),
         ],
-        compiler_params=pltpu.CompilerParams(vmem_limit_bytes=24 * 2**20),
+        compiler_params=pltpu.CompilerParams(vmem_limit_bytes=32 * 2**20),
         name="substeps",
     )(*laid)
-    return tuple(x.reshape((levels, height, width)) for x in news)
+    return tuple(news)
 
 
 def solution(mesh):

time: 87.2 us -> 30 us (0.34)
  Pallas kernels: 86.4 us -> 29.2 us
    pallas_call x2, Pallas kernels: 86.4 us -> 29.2 us  [the longest x1 15.6 us: on_device(): pl.pallas_call(exchange, out_shape=(pltpu.VMEM((4, levels, deep, width),...]
where the time goes in v5:
time: 30 us; the launch traced here: 29.9 us
  Pallas kernels  29.2 us (97%)
  between operations  0.64 us (2%)
    pallas_call x1, Pallas kernels, on_device(): pl.pallas_call(exchange, out_shape=(pltpu.VMEM((4, levels, deep, width),...  15.6 us
    pallas_call x1, Pallas kernels, on_device(): pl.pallas_call(substeps, out_shape=(jax.ShapeDtypeStruct((levels, height,...  13.6 us

profile of v5, /device:TPU:0, one launch (start us, length us, event | category | flops | bytes accessed | tf_op | source)
XLA Modules:
  0.0 29.9 jit_solution(16011218411745004696)
XLA Ops:
  0.6 15.6 %exchange.1 = (f32[4,16,72,128]{3,2,1,0:T(8,128)S(1)}, f32[6,72,128]{2,1,0:T(8,128)S(1)}, f32[2,4,72,128]{3,2,1,0:T(8,128)S(1)}, f32[2,6,72,128]{3,2,1,0:T(8,128)S(1)}, f32[2,17,8,128]{3,2,1,0:T(8,128)S(1)}) custom-call(f32[1024,128]{1,0:T(8,128)} %bitcast.4, f32[1024,128]{1,0:T(8,128)} %bitcast.5, f32[1024,128]{1,0:T(8,128)} %bitcast.6, ...), custom_call_target="tpu_custom_call" | custom-call | tf_op jit(solution)/shard_map/exchange/pallas_call | solution.py:471
  16.2 13.6 %substeps.1 = (f32[16,64,128]{2,1,0:T(8,128)}, f32[16,64,128]{2,1,0:T(8,128)}, f32[16,64,128]{2,1,0:T(8,128)}, f32[16,64,128]{2,1,0:T(8,128)}) custom-call(f32[4,16,72,128]{3,2,1,0:T(8,128)S(1)} %get-tuple-element.9.state, f32[6,72,128]{2,1,0:T(8,128)S(1)} %get-tuple-element.10.table, f32[2,4,72,128]{3,2,1,0:T(8,128)S(1)} %get-tuple-element.11.sides, ...), custom_call_target="tpu_custom_call" | custom-call | tf_op jit(solution)/shard_map/substeps/pallas_call | solution.py:510

commit v6 on v5

--- a/solution.py
+++ b/solution.py
@@ -74,15 +74,12 @@
     row = lax.broadcasted_iota(jnp.int32, (8, width), 0)
     group = lane // 8
     within = lane - group * 8
-    for load in loads:
-        load.wait()
-
-    @pl.loop(0, height // 8)
-    def _(tile):
+
+    def pack(pair, tile):
         start = pl.multiple_of(tile * 8, 8)
         rows = pl.ds(start, 8)
         cols = []
-        for f in range(4):
+        for f in (2 * pair, 2 * pair + 1):
             acc = pltpu.roll(field[f, rows, :], 8 * (levels - 1) + RIM, 1)
             for level in range(1, levels):
                 spot = levels - 1 - level
@@ -90,18 +87,31 @@
                 acc = jnp.where(group == spot, pltpu.roll(field[f, at, :], 8 * spot + RIM, 1), acc)
             packed[f, rows, :] = acc
             cols.append(acc)
-        acc = jnp.zeros((8, width), jnp.float32)
-        raw = (bath[rows, :].astype(jnp.float32), whole[0, rows, :], whole[1, rows, :], whole[2, rows, :])
-        for m in range(4):
-            metric[m, rows, :] = raw[m]
-            acc = jnp.where(group == m, pltpu.roll(raw[m], 8 * m + RIM, 1), acc)
-        packed[4, rows, :] = acc
-        for pair in range(2):
-            one, two = cols[2 * pair], cols[2 * pair + 1]
-            to_side[0, pair, rows, :] = jnp.where(within < 4, one, pltpu.roll(two, 4, 1))
-            to_side[1, pair, rows, :] = jnp.where(within < 3, pltpu.roll(two, width - 3, 1), one)
-        to_side[0, 2, rows, :] = acc
-        to_side[1, 2, rows, :] = acc
+        if pair == 0:
+            acc = jnp.zeros((8, width), jnp.float32)
+            raw = (bath[rows, :].astype(jnp.float32), whole[0, rows, :], whole[1, rows, :], whole[2, rows, :])
+            for m in range(4):
+                metric[m, rows, :] = raw[m]
+                acc = jnp.where(group == m, pltpu.roll(raw[m], 8 * m + RIM, 1), acc)
+            packed[4, rows, :] = acc
+            extra_w = pltpu.roll(acc, 3, 1)
+            extra_e = jnp.where(within == 3, extra_w, pltpu.roll(acc, 6, 1))
+        else:
+            extra_e = extra_w = pltpu.roll(packed[4, rows, :], 1, 1)
+        one, two = cols
+        to_side[0, pair, rows, :] = jnp.where(
+            within < 3, one, jnp.where((within == 3) | (within == 7), extra_e, pltpu.roll(two, 4, 1))
+        )
+        to_side[1, pair, rows, :] = jnp.where(
+            within < 3, pltpu.roll(two, width - 3, 1), jnp.where(within < 6, one, extra_w)
+        )
+
+    for at in (0, 1, 4, 5, 6, 7):
+        loads[at].wait()
+
+    @pl.loop(0, height // 8)
+    def _(tile):
+        pack(0, tile)
 
     @pl.when(lat > 0)
     def _():
@@ -117,10 +127,21 @@
             device_id=peer, device_id_type=MESH,
         )
 
-    go_east = remote(to_side.at[0], from_side.at[0], 0, 0, east)
-    go_west = remote(to_side.at[1], from_side.at[1], 1, 1, west)
-    go_east.start()
-    go_west.start()
+    across = []
+    for pair in range(2):
+        across.append(remote(to_side.at[0, pair], from_side.at[0, pair], 6 * pair, 6 * pair, east))
+        across.append(remote(to_side.at[1, pair], from_side.at[1, pair], 6 * pair + 1, 6 * pair + 1, west))
+    across[0].start()
+    across[1].start()
+    for at in (2, 3, 8, 9):
+        loads[at].wait()
+
+    @pl.loop(0, height // 8)
+    def _(tile):
+        pack(1, tile)
+
+    across[2].start()
+    across[3].start()
 
     def column(f, r, half):
         return field[f, pl.ds(r + half * 8 * height, 8, stride=height), :]
@@ -186,13 +207,13 @@
         for m in range(6):
             table[m, rows, :] = made[m]
 
-    go_east.wait_recv()
-    go_west.wait_recv()
+    for copy in across:
+        copy.wait_recv()
 
     @pl.loop(0, height // 8)
     def _(tile):
         rows = pl.ds(pl.multiple_of(tile * 8, 8), 8)
-        for f in range(5):
+        for f in range(4):
             own = packed[f, rows, :]
             got_w = from_side[0, f // 2, rows, :]
             got_e = from_side[1, f // 2, rows, :]
@@ -201,6 +222,17 @@
                 got_e = pltpu.roll(got_e, 3, 1)
             strips[0, f, rows, :] = jnp.where(within < RIM, got_w, own)
             strips[1, f, rows, :] = jnp.where(within < RIM, own, got_e)
+        own = packed[4, rows, :]
+        first, second = from_side[0, 0, rows, :], from_side[0, 1, rows, :]
+        got_w = jnp.where(
+            within == 0,
+            pltpu.roll(first, width - 3, 1),
+            jnp.where(within == 1, pltpu.roll(first, width - 6, 1), pltpu.roll(second, width - 1, 1)),
+        )
+        first, second = from_side[1, 0, rows, :], from_side[1, 1, rows, :]
+        got_e = jnp.where(within < 5, pltpu.roll(first, width - 3, 1), pltpu.roll(second, width - 1, 1))
+        strips[0, 4, rows, :] = jnp.where(within < RIM, got_w, own)
+        strips[1, 4, rows, :] = jnp.where((within < RIM) | (within > 5), own, got_e)
 
     edge_n[30:32, :] = jnp.zeros((2, width), jnp.float32)
     edge_s[30:32, :] = jnp.zeros((2, width), jnp.float32)
@@ -247,8 +279,8 @@
     def _(tile):
         side_tables(pl.ds(pl.multiple_of(tile * 8, 8), 8))
 
-    go_east.wait_send()
-    go_west.wait_send()
+    for copy in across:
+        copy.wait_send()
     rows_in(*main)
 
     def mirrored(value, index):
@@ -353,7 +385,7 @@
             results.append(new)
         return results
 
-    def main_step(source, store, count):
+    def main_step(source, store, count, after=None):
         @pl.loop(0, levels)
         def _(level):
             number = level.astype(jnp.float32)
@@ -381,6 +413,8 @@
                 new = update(centre, easts, wests, norths, souths, factor, number, mix)
                 for f in range(4):
                     store(f, level, t, new[f])
+            if after is not None:
+                after(level)
 
     def side_step(source, target):
         mix = (mixing[0, levels], mixing[1, levels])
@@ -437,14 +471,14 @@
     main_step(second, into(third), tiles)
     side_step(sides_second, sides_third)
     join(sides_third)
-    main_step(third, final, tiles - 1)
-    stores = [
-        pltpu.make_async_copy(result.at[f], outs[f], store_sem.at[f]) for f in range(4)
-    ]
-    for copy in stores:
-        copy.start()
-    for copy in stores:
-        copy.wait()
+
+    def leave(level):
+        for f in range(4):
+            pltpu.make_async_copy(result.at[f, level], outs[f].at[level], store_sem.at[f]).start()
+
+    main_step(third, final, tiles - 1, leave)
+    for f in range(4):
+        pltpu.make_async_copy(result.at[f], outs[f], store_sem.at[f]).wait()
 
 
 def on_device(
@@ -494,12 +528,12 @@
             pltpu.VMEM((message, width), f32),
             pltpu.VMEM((message, width), f32),
             pltpu.VMEM((5, height, width), f32),
-            pltpu.VMEM((2, 3, height, width), f32),
-            pltpu.VMEM((2, 3, height, width), f32),
+            pltpu.VMEM((2, 2, height, width), f32),
+            pltpu.VMEM((2, 2, height, width), f32),
             pltpu.VMEM((32, width), f32),
             pltpu.VMEM((32, width), f32),
-            pltpu.SemaphoreType.DMA((6,)),
-            pltpu.SemaphoreType.DMA((6,)),
+            pltpu.SemaphoreType.DMA((8,)),
+            pltpu.SemaphoreType.DMA((8,)),
             pltpu.SemaphoreType.DMA((10,)),
         ],
         compiler_params=pltpu.CompilerParams(

time: 30 us -> 28.9 us (0.963)
  Pallas kernels: 29.2 us -> 28.1 us
    pallas_call x1, Pallas kernels: 13.6 us -> 13 us  [on_device(): pl.pallas_call(substeps, out_shape=(jax.ShapeDtypeStruct((levels, height,...]
    pallas_call x1, Pallas kernels: 15.6 us -> 15.1 us  [on_device(): pl.pallas_call(exchange, out_shape=(pltpu.VMEM((4, levels, deep, width),...]
where the time goes in v6:
time: 28.9 us; the launch traced here: 28.8 us
  Pallas kernels  28.1 us (97%)
  between operations  0.64 us (2%)
    pallas_call x1, Pallas kernels, on_device(): pl.pallas_call(exchange, out_shape=(pltpu.VMEM((4, levels, deep, width),...  15.1 us
    pallas_call x1, Pallas kernels, on_device(): pl.pallas_call(substeps, out_shape=(jax.ShapeDtypeStruct((levels, height,...  13 us

profile of v6, /device:TPU:0, one launch (start us, length us, event | category | flops | bytes accessed | tf_op | source)
XLA Modules:
  0.0 28.8 jit_solution(7337691949480980322)
XLA Ops:
  0.6 15.1 %exchange.1 = (f32[4,16,72,128]{3,2,1,0:T(8,128)S(1)}, f32[6,72,128]{2,1,0:T(8,128)S(1)}, f32[2,4,72,128]{3,2,1,0:T(8,128)S(1)}, f32[2,6,72,128]{3,2,1,0:T(8,128)S(1)}, f32[2,17,8,128]{3,2,1,0:T(8,128)S(1)}) custom-call(f32[1024,128]{1,0:T(8,128)} %bitcast.4, f32[1024,128]{1,0:T(8,128)} %bitcast.5, f32[1024,128]{1,0:T(8,128)} %bitcast.6, ...), custom_call_target="tpu_custom_call" | custom-call | tf_op jit(solution)/shard_map/exchange/pallas_call | solution.py:505
  15.7 13.0 %substeps.1 = (f32[16,64,128]{2,1,0:T(8,128)}, f32[16,64,128]{2,1,0:T(8,128)}, f32[16,64,128]{2,1,0:T(8,128)}, f32[16,64,128]{2,1,0:T(8,128)}) custom-call(f32[4,16,72,128]{3,2,1,0:T(8,128)S(1)} %get-tuple-element.9.state, f32[6,72,128]{2,1,0:T(8,128)S(1)} %get-tuple-element.10.table, f32[2,4,72,128]{3,2,1,0:T(8,128)S(1)} %get-tuple-element.11.sides, ...), custom_call_target="tpu_custom_call" | custom-call | tf_op jit(solution)/shard_map/substeps/pallas_call | solution.py:544

commit v7 on v6

--- a/solution.py
+++ b/solution.py
@@ -386,6 +386,8 @@
         return results
 
     def main_step(source, store, count, after=None):
+        flat = source.reshape(4, levels * deep, width)
+
         @pl.loop(0, levels)
         def _(level):
             number = level.astype(jnp.float32)
@@ -400,12 +402,12 @@
                     easts.append(pltpu.roll(jnp.where(lane == 0, z, c), width - 1, 1))
                     wests.append(pltpu.roll(jnp.where(lane == width - 1, z, c), 1, 1))
                     if t < tiles - 1:
-                        norths.append(source[f, level, 8 * t + 1 : 8 * t + 9, :])
+                        norths.append(flat[f, pl.ds(level * deep + 8 * t + 1, 8), :])
                     else:
                         wrapped = pltpu.roll(source[f, level, 0:8, :], 7, 0)
                         norths.append(jnp.where(row == 7, wrapped, pltpu.roll(c, 7, 0)))
                     if t > 0:
-                        souths.append(source[f, level, 8 * t - 1 : 8 * t + 7, :])
+                        souths.append(flat[f, pl.ds(level * deep + 8 * t - 1, 8), :])
                     else:
                         wrapped = pltpu.roll(source[f, level, deep - 8 : deep, :], 1, 0)
                         souths.append(jnp.where(row == 0, wrapped, pltpu.roll(c, 1, 0)))

time: 28.9 us -> 28.9 us (level)
  no operation moved by 1% of the time
where the time goes in v7:
time: 28.9 us; the launch traced here: 28.8 us
  Pallas kernels  28.1 us (97%)
  between operations  0.64 us (2%)
    pallas_call x1, Pallas kernels, on_device(): pl.pallas_call(exchange, out_shape=(pltpu.VMEM((4, levels, deep, width),...  15.1 us
    pallas_call x1, Pallas kernels, on_device(): pl.pallas_call(substeps, out_shape=(jax.ShapeDtypeStruct((levels, height,...  13 us

profile of v7, /device:TPU:0, one launch (start us, length us, event | category | flops | bytes accessed | tf_op | source)
XLA Modules:
  0.0 28.8 jit_solution(12178730331124944352)
XLA Ops:
  0.6 15.1 %exchange.1 = (f32[4,16,72,128]{3,2,1,0:T(8,128)S(1)}, f32[6,72,128]{2,1,0:T(8,128)S(1)}, f32[2,4,72,128]{3,2,1,0:T(8,128)S(1)}, f32[2,6,72,128]{3,2,1,0:T(8,128)S(1)}, f32[2,17,8,128]{3,2,1,0:T(8,128)S(1)}) custom-call(f32[1024,128]{1,0:T(8,128)} %bitcast.4, f32[1024,128]{1,0:T(8,128)} %bitcast.5, f32[1024,128]{1,0:T(8,128)} %bitcast.6, ...), custom_call_target="tpu_custom_call" | custom-call | tf_op jit(solution)/shard_map/exchange/pallas_call | solution.py:507
  15.7 13.0 %substeps.1 = (f32[16,64,128]{2,1,0:T(8,128)}, f32[16,64,128]{2,1,0:T(8,128)}, f32[16,64,128]{2,1,0:T(8,128)}, f32[16,64,128]{2,1,0:T(8,128)}) custom-call(f32[4,16,72,128]{3,2,1,0:T(8,128)S(1)} %get-tuple-element.9.state, f32[6,72,128]{2,1,0:T(8,128)S(1)} %get-tuple-element.10.table, f32[2,4,72,128]{3,2,1,0:T(8,128)S(1)} %get-tuple-element.11.sides, ...), custom_call_target="tpu_custom_call" | custom-call | tf_op jit(solution)/shard_map/substeps/pallas_call | solution.py:546

commit v8 on v6

--- a/solution.py
+++ b/solution.py
@@ -395,10 +395,10 @@
                 centre, easts, wests, norths, souths = [], [], [], [], []
                 for f in range(4):
                     c = source[f, level, rows, :]
-                    z = pltpu.roll(link[f, rows, :], width - 3 - 8 * (levels - 1) + 8 * level, 1)
+                    z = pltpu.roll(link[f, rows, :], width - 2 - 8 * (levels - 1) + 8 * level, 1)
                     centre.append(c)
-                    easts.append(pltpu.roll(jnp.where(lane == 0, z, c), width - 1, 1))
-                    wests.append(pltpu.roll(jnp.where(lane == width - 1, z, c), 1, 1))
+                    easts.append(jnp.where(lane == width - 1, z, pltpu.roll(c, width - 1, 1)))
+                    wests.append(jnp.where(lane == 0, z, pltpu.roll(c, 1, 1)))
                     if t < tiles - 1:
                         norths.append(source[f, level, 8 * t + 1 : 8 * t + 9, :])
                     else:
@@ -454,7 +454,8 @@
         def _(t):
             rows = pl.ds(pl.multiple_of(t * 8, 8), 8)
             for f in range(4):
-                link[f, rows, :] = jnp.where(within == 2, source[0, f, rows, :], source[1, f, rows, :])
+                beyond = pltpu.roll(source[1, f, rows, :], width - 2, 1)
+                link[f, rows, :] = jnp.where(within == 2, source[0, f, rows, :], beyond)
 
     def into(buffer):
         def store(f, level, t, value):

time: 28.9 us -> 29.2 us (1.010)
  Pallas kernels: 28.1 us -> 28.5 us
    pallas_call x1, Pallas kernels: 13 us -> 13.4 us  [on_device(): pl.pallas_call(substeps, out_shape=(jax.ShapeDtypeStruct((levels, height,...]
where the time goes in v8:
time: 29.2 us; the launch traced here: 29.1 us
  Pallas kernels  28.5 us (98%)
  between operations  0.64 us (2%)
    pallas_call x1, Pallas kernels, on_device(): pl.pallas_call(exchange, out_shape=(pltpu.VMEM((4, levels, deep, width),...  15.1 us
    pallas_call x1, Pallas kernels, on_device(): pl.pallas_call(substeps, out_shape=(jax.ShapeDtypeStruct((levels, height,...  13.4 us

profile of v8, /device:TPU:0, one launch (start us, length us, event | category | flops | bytes accessed | tf_op | source)
XLA Modules:
  0.0 29.1 jit_solution(14570519562336639221)
XLA Ops:
  0.6 15.1 %exchange.1 = (f32[4,16,72,128]{3,2,1,0:T(8,128)S(1)}, f32[6,72,128]{2,1,0:T(8,128)S(1)}, f32[2,4,72,128]{3,2,1,0:T(8,128)S(1)}, f32[2,6,72,128]{3,2,1,0:T(8,128)S(1)}, f32[2,17,8,128]{3,2,1,0:T(8,128)S(1)}) custom-call(f32[1024,128]{1,0:T(8,128)} %bitcast.4, f32[1024,128]{1,0:T(8,128)} %bitcast.5, f32[1024,128]{1,0:T(8,128)} %bitcast.6, ...), custom_call_target="tpu_custom_call" | custom-call | tf_op jit(solution)/shard_map/exchange/pallas_call | solution.py:506
  15.7 13.4 %substeps.1 = (f32[16,64,128]{2,1,0:T(8,128)}, f32[16,64,128]{2,1,0:T(8,128)}, f32[16,64,128]{2,1,0:T(8,128)}, f32[16,64,128]{2,1,0:T(8,128)}) custom-call(f32[4,16,72,128]{3,2,1,0:T(8,128)S(1)} %get-tuple-element.9.state, f32[6,72,128]{2,1,0:T(8,128)S(1)} %get-tuple-element.10.table, f32[2,4,72,128]{3,2,1,0:T(8,128)S(1)} %get-tuple-element.11.sides, ...), custom_call_target="tpu_custom_call" | custom-call | tf_op jit(solution)/shard_map/substeps/pallas_call | solution.py:545
